TPU v7x, 32 devices: a whole 2x2x4 slice. The times are simulated.
32 devices in a mesh: dp: 16 (over z, y, x), mp: 2 (over core).
Axes of the slice: x: 2, y: 2, z: 4, core: 2. Of those that a mesh axis runs over, the one named last changes fastest.
Arguments:
- query_states: bfloat16 [512, 4096], P('dp')
- passage_states: bfloat16 [4096, 4096], P('dp')
- head_weight: bfloat16 [4096, 2048], P(None, 'mp'), may hold values from -0.09375 to 0.09375
- positives: int32 [512], P('dp'), may hold values from 0 to 4095, as said below
- negatives: int32 [512, 8], P('dp'), may hold values from 0 to 4095, as said below
- search_cost_incoming_slope: float32 [512], P('dp'), may hold values from 20 to 200
Outputs:
- losses: float32 [512], P('dp')
- query_grads: bfloat16 [512, 4096], P('dp', 'mp')
- passage_grads: bfloat16 [4096, 4096], P('dp', 'mp')
Inputs may be any that keep to these rules, and one draw needn't show every extreme that they name: `positives`: the queries of one aligned block of 32 rows name, over their positive and hard negatives together, at most 36 passages of any one aligned block of 256 passages (repeats counted); in every draw one block of passages is named exactly 36 times by the queries of every block. `negatives`: see positives: the bound counts both arguments together.
All inputs are finite; a program needn't handle non-finite values.
Results may differ from a plain program's by a relative error of at most 0.015.
Values may be sent and summed in bfloat16 or wider, within the bound.
A program may use at most 128 MiB of HBM per device.

v0:
```python
import jax
import jax.numpy as jnp
from jax import lax
from jax.sharding import PartitionSpec as P

sharpness_divisor = 0.02


def tangent(unit_rows, inv_norm, upstream, radial):
    return (inv_norm * (upstream - unit_rows * radial[:, None])).astype(jnp.bfloat16)


def per_device(
    query_states, passage_states, head_weight, positives, negatives, search_cost_incoming_slope
):
    q_rows = query_states.shape[0]
    p_rows = passage_states.shape[0]
    width = head_weight.shape[1]
    devices = lax.axis_size("dp")
    position = lax.axis_index("dp")
    q_proj = jnp.dot(query_states, head_weight, preferred_element_type=jnp.float32)
    p_proj = jnp.dot(passage_states, head_weight, preferred_element_type=jnp.float32)
    q_square, p_square = lax.psum(
        (jnp.sum(q_proj * q_proj, axis=1), jnp.sum(p_proj * p_proj, axis=1)), "mp"
    )
    q_inv = lax.rsqrt(q_square + 1e-06)[:, None]
    p_inv = lax.rsqrt(p_square + 1e-06)[:, None]
    q_unit = q_proj * q_inv
    p_unit = p_proj * p_inv
    search_embedding_matrix = q_unit.astype(jnp.bfloat16)
    p_embed = p_unit.astype(jnp.bfloat16)
    asked_ids = jnp.concatenate([positives[:, None], negatives], axis=1).reshape(-1)
    requests = asked_ids.shape[0]
    per_query = negatives.shape[1] + 1
    capacity = max(4, 2 * requests // devices)
    owners = asked_ids // p_rows
    local_row = asked_ids % p_rows
    positions = jnp.arange(requests)
    earlier = jnp.sum(
        (owners[None, :] == owners[:, None]) & (positions[None, :] < positions[:, None]), axis=1
    )
    slot_index = owners * capacity + earlier
    outgoing = jnp.full((devices * capacity,), -1, jnp.int32).at[slot_index].set(local_row)
    outgoing = outgoing.reshape(devices, capacity)
    asked_rows = lax.all_to_all(outgoing, "dp", split_axis=0, concat_axis=0, tiled=True)
    is_valid = asked_rows >= 0
    picked_rows = jnp.where(
        is_valid[:, :, None], p_embed[jnp.maximum(asked_rows, 0)], jnp.zeros((), jnp.bfloat16)
    )
    returned = lax.all_to_all(picked_rows, "dp", split_axis=0, concat_axis=0, tiled=True)
    replies, asked_rows = (returned, asked_rows)
    fetched = replies.reshape(devices * capacity, width)[slot_index].reshape(
        q_rows, per_query, width
    )
    matching_document_matrix = fetched[:, 0]
    distractor_embedding_matrix = fetched[:, 1:]
    batch_pos = lax.all_gather(matching_document_matrix, "dp", axis=0, tiled=True)
    contract_rows = (((1,), (1,)), ((), ()))
    batch_part = lax.dot_general(
        search_embedding_matrix, batch_pos, contract_rows, preferred_element_type=jnp.float32
    )
    hard_part = jnp.einsum(
        "bm,bgm->bg",
        search_embedding_matrix,
        distractor_embedding_matrix,
        preferred_element_type=jnp.float32,
    )
    sibling_document_similarity, fetched_distractor_similarity = lax.psum(
        (batch_part, hard_part), "mp"
    )
    sibling_document_similarity = sibling_document_similarity / sharpness_divisor
    fetched_distractor_similarity = fetched_distractor_similarity / sharpness_divisor
    columns = jnp.arange(sibling_document_similarity.shape[1])
    own_columns = position * q_rows + jnp.arange(q_rows)
    self_match_filter = columns[None, :] == own_columns[:, None]
    log_total = jnp.log(
        jnp.sum(jnp.exp(sibling_document_similarity), axis=1)
        + jnp.sum(jnp.exp(fetched_distractor_similarity), axis=1)
    )
    losses = log_total - jnp.sum(
        jnp.where(self_match_filter, sibling_document_similarity, 0.0), axis=1
    )
    sibling_document_likelihood = jnp.exp(sibling_document_similarity - log_total[:, None])
    fetched_distractor_likelihood = jnp.exp(fetched_distractor_similarity - log_total[:, None])
    sibling_document_slope = (
        search_cost_incoming_slope[:, None]
        * (sibling_document_likelihood - self_match_filter.astype(jnp.float32))
        / sharpness_divisor
    ).astype(jnp.bfloat16)
    fetched_distractor_slope = (
        search_cost_incoming_slope[:, None] * fetched_distractor_likelihood / sharpness_divisor
    )
    q_grad = jnp.dot(sibling_document_slope, batch_pos, preferred_element_type=jnp.float32)
    q_grad = q_grad + jnp.einsum(
        "qk,qke->qe",
        fetched_distractor_slope,
        distractor_embedding_matrix.astype(jnp.float32),
        precision=lax.Precision.HIGHEST,
    )
    contract_first = (((0,), (0,)), ((), ()))
    pos_grad = lax.psum_scatter(
        lax.dot_general(
            sibling_document_slope,
            search_embedding_matrix,
            contract_first,
            preferred_element_type=jnp.float32,
        ),
        "dp",
        scatter_dimension=0,
        tiled=True,
    )
    neg_grad = (
        fetched_distractor_slope[:, :, None]
        * search_embedding_matrix.astype(jnp.float32)[:, None, :]
    )
    slot_grads = jnp.concatenate([pos_grad[:, None], neg_grad], axis=1).reshape(requests, width)
    outgoing_grads = (
        jnp.zeros((devices * capacity, width), jnp.float32).at[slot_index].set(slot_grads)
    )
    incoming = lax.all_to_all(
        outgoing_grads.reshape(devices, capacity, width).astype(jnp.bfloat16),
        "dp",
        split_axis=0,
        concat_axis=0,
        tiled=True,
    ).astype(jnp.float32)
    is_valid = asked_rows >= 0
    incoming = jnp.where(is_valid[:, :, None], incoming, 0.0).reshape(-1, width)
    p_grad = (
        jnp.zeros((p_rows, width), jnp.float32)
        .at[jnp.maximum(asked_rows, 0).reshape(-1)]
        .add(incoming)
    )
    q_radial, p_radial = lax.psum(
        (jnp.sum(q_unit * q_grad, axis=1), jnp.sum(p_unit * p_grad, axis=1)), "mp"
    )
    q_dir = tangent(q_unit, q_inv, q_grad, q_radial)
    p_dir = tangent(p_unit, p_inv, p_grad, p_radial)
    q_state = lax.dot_general(q_dir, head_weight, contract_rows, preferred_element_type=jnp.float32)
    p_state = lax.dot_general(p_dir, head_weight, contract_rows, preferred_element_type=jnp.float32)
    query_grads, passage_grads = (
        lax.psum_scatter(
            q_state.astype(jnp.bfloat16), "mp", scatter_dimension=1, tiled=True
        ).astype(jnp.float32),
        lax.psum_scatter(
            p_state.astype(jnp.bfloat16), "mp", scatter_dimension=1, tiled=True
        ).astype(jnp.float32),
    )
    return (losses, query_grads.astype(jnp.bfloat16), passage_grads.astype(jnp.bfloat16))


def solution(mesh):
    placed = (P("dp", None), P("dp", None), P(None, "mp"), P("dp"), P("dp", None), P("dp"))
    return jax.shard_map(
        per_device,
        mesh=mesh,
        in_specs=placed,
        out_specs=(P("dp"), P("dp", "mp"), P("dp", "mp")),
        check_vma=False,
    )
```

profile of v0, /device:TPU:0, one launch (start us, length us, event | category | flops | bytes accessed | tf_op | source)
XLA Modules:
  0.0 335.6 jit_solution(11049418453858072877)
XLA Ops:
  7.2 0.8 pad_add_fusion
  8.3 0.2 convert_reduce_fusion
  8.6 2.9 scatter_custom_fusion
  11.5 0.7 all_to_all.12
  12.2 8.3 %all-to-all-start = ((s32[16,1,36]{2,1,0:T(1,128)}), s32[16,1,36]{2,1,0:T(1,128)S(1)}, u32[]{:S(2)}, u32[]{:S(2)}) async-start(s32[16,1,36]{2,1,0:T(1,128)} %all_to_all.12), calls=%async_computation | async-start | bytes 16384 | tf_op jit(solution)/shard_map/all_to_all | solution.py:45
  20.6 5.3 %multiply_reduce_fusion.3 = (f32[32]{0:T(128)S(1)}, f32[32,1024]{1,0:T(8,128)S(1)}) fusion(bf16[32,4096]{1,0:T(8,128)(2,1)} %param.6, bf16[4096,1024]{1,0:T(8,128)(2,1)} %param.8), kind=kOutput, calls=%fused_computation.35 | convolution fusion | flops 268500960 | bytes 8781952 | tf_op jit(solution)/shard_map/dot_general | solution.py:21
  25.8 0.6 copy-done.1
  26.4 3.4 %multiply_reduce_fusion.1 = (f32[256]{0:T(256)S(1)}, f32[256,1024]{1,0:T(8,128)}) fusion(bf16[256,4096]{1,0:T(8,128)(2,1)S(1)} %copy-done, bf16[4096,1024]{1,0:T(8,128)(2,1)S(1)} %copy-done.1), kind=kOutput, calls=%fused_computation.18 | convolution fusion | flops 2148007680 | bytes 11535360 | tf_op jit(solution)/shard_map/dot_general | solution.py:22
  29.8 2.4 all-reduce.1
  32.3 1.4 multiply_convert_fusion.1
  33.8 0.6 copy-done.6
  34.4 3.4 %gather_fusion = bf16[576,1024]{1,0:T(8,128)(2,1)} fusion(bf16[256,1024]{1,0:T(8,128)(2,1)S(1)} %multiply_convert_fusion.1, s32[1024]{0:T(1024)S(1)} %pad_clamp_fusion.1), kind=kCustom, calls=%fused_computation | custom fusion | bytes 2361600 | tf_op jit(solution)/shard_map/gather | solution.py:48
  37.8 1.4 reshape.212
  39.1 1.2 broadcast_select_fusion
  40.4 6.9 %all-to-all-start.1 = ((bf16[16,36,1024]{2,1,0:T(8,128)(2,1)}), bf16[16,36,1024]{2,1,0:T(8,128)(2,1)}, u32[]{:S(2)}, u32[]{:S(2)}) async-start(bf16[16,36,1024]{2,1,0:T(8,128)(2,1)} %broadcast_select_fusion), calls=%async_computation.1 | async-start | bytes 2621440 | tf_op jit(solution)/shard_map/all_to_all | solution.py:50
  47.4 29.6 %all-to-all-done.1 = bf16[16,36,1024]{2,1,0:T(8,128)(2,1)} async-done(((bf16[16,36,1024]{2,1,0:T(8,128)(2,1)}), bf16[16,36,1024]{2,1,0:T(8,128)(2,1)}, u32[]{:S(2)}, u32[]{:S(2)}) %all-to-all-start.1) | async-done | bytes 1179680 | tf_op jit(solution)/shard_map/all_to_all | solution.py:50
  77.0 1.4 reshape.207
  78.4 2.6 gather_fusion.1
  81.0 1.3 reshape.208
  82.4 0.8 copy.27
  83.4 0.4 fusion.11
  83.9 3.4 %psum.45 = f32[32,8]{1,0:T(8,128)S(1)} all-reduce(f32[32,8]{1,0:T(8,128)S(1)} %bitcast.39), channel_id=1, replica_groups=mesh['dp'=16,'mp'=2] {'mp'}, use_global_device_ids=true, to_apply=%region_8.9 | all-reduce | flops 256 | bytes 2048 | tf_op jit(solution)/shard_map/psum | solution.py:68
  87.2 53.0 %all-gather.3.cloned.1.call-done = bf16[512,1,1024]{2,0,1:T(8,128)(2,1)} async-done(((bf16[32,1,1024]{2,0,1:T(8,128)(2,1)}), bf16[512,1,1024]{2,0,1:T(8,128)(2,1)}) %all-gather.3.cloned.1.call-update) | async-done | bytes 1048592 | tf_op jit(solution)/shard_map/all_gather | solution.py:57
  140.2 2.3 fusion.3
  142.7 16.9 %all-reduce.4.cloned.1.call-done = f32[32,512]{1,0:T(8,128)} async-done(((f32[32,512]{1,0:T(8,128)}), f32[32,512]{1,0:T(8,128)}) %all-reduce.4.cloned.1.call-update) | async-done | bytes 65552 | tf_op jit(solution)/shard_map/psum | solution.py:68
  159.6 1.0 select_reduce_fusion
  160.6 0.5 fusion.23
  161.2 2.7 fusion.21
  164.0 0.1 broadcast_multiply_fusion
  164.2 81.7 %reduce-scatter.6.cloned.1.call-done = f32[32,1024]{1,0:T(8,128)} async-done(((f32[512,1024]{1,0:T(8,128)}), f32[32,1024]{1,0:T(8,128)}) %reduce-scatter.6.cloned.1.call-update) | async-done | bytes 131088 | tf_op jit(solution)/shard_map/reduce_scatter | solution.py:101
  245.9 1.0 copy.28
  246.9 1.7 pad_maximum_fusion
  248.6 1.6 reshape.239
  250.2 3.2 scatter_custom_fusion.1
  253.4 1.8 convert_element_type.52
  255.2 1.2 convert_element_type.53
  256.4 3.9 %all-to-all-start.2 = ((bf16[16,36,1024]{2,1,0:T(8,128)(2,1)}), bf16[16,36,1024]{2,1,0:T(8,128)(2,1)S(1)}, u32[]{:S(2)}, u32[]{:S(2)}) async-start(bf16[16,36,1024]{2,1,0:T(8,128)(2,1)} %convert_element_type.53), calls=%async_computation.4 | async-start | bytes 2621440 | tf_op jit(solution)/shard_map/all_to_all | solution.py:120
  260.4 1.8 fusion.9
  262.2 2.4 multiply_reduce_fusion.2
  264.6 16.6 %all-to-all-done.2 = bf16[16,36,1024]{2,1,0:T(8,128)(2,1)S(1)} async-done(((bf16[16,36,1024]{2,1,0:T(8,128)(2,1)}), bf16[16,36,1024]{2,1,0:T(8,128)(2,1)S(1)}, u32[]{:S(2)}, u32[]{:S(2)}) %all-to-all-start.2) | async-done | bytes 1179680 | tf_op jit(solution)/shard_map/all_to_all | solution.py:120
  281.1 2.4 convert_select_fusion
  283.6 2.9 reshape.247
  286.5 11.3 %scatter_custom_fusion.2 = f32[256,1024]{1,0:T(8,128)} fusion(s32[576]{0:T(1024)} %copy-done.6, f32[576,1024]{1,0:T(8,128)} %reshape.247, f32[]{:T(128)} %constant.26.clone.1), kind=kCustom, calls=%fused_computation.22 | custom fusion | flops 589824 | bytes 1049088 | tf_op jit(solution)/shard_map/scatter-add | solution.py:132
  297.8 1.5 multiply_reduce_fusion
  299.3 2.5 all-reduce
  301.8 6.7 %convolution_convert_fusion.1 = bf16[32,4096]{1,0:T(8,128)(2,1)} fusion(bf16[4096,1024]{1,0:T(8,128)(2,1)} %param.8, f32[32,1024]{1,0:T(8,128)S(1)} %copy-done.4, f32[32,1024]{1,0:T(8,128)S(1)} %get-tuple-element.16, f32[32]{0:T(128)S(1)} %get-tuple-element.5, f32[32]{0:T(128)S(1)} %copy-done.13), kind=kOutput, calls=%fused_computation.6 | convolution fusion | flops 268730368 | bytes 8913152 | tf_op jit(solution)/shard_map/dot_general | solution.py:139
  308.5 7.5 %convolution_convert_fusion = bf16[256,4096]{1,0:T(8,128)(2,1)} fusion(bf16[4096,1024]{1,0:T(8,128)(2,1)} %param.8, f32[256,1024]{1,0:T(8,128)} %scatter_custom_fusion.2, f32[256,1024]{1,0:T(8,128)S(1)} %copy-done.2, f32[256]{0:T(256)S(1)} %get-tuple-element.6, f32[256]{0:T(256)S(1)} %copy-done.8), kind=kOutput, calls=%fused_computation.5 | convolution fusion | flops 2149842944 | bytes 12584960 | tf_op jit(solution)/shard_map/dot_general | solution.py:140
  316.1 12.9 %reduce-scatter.8.cloned.1.call-done = bf16[256,2048]{1,0:T(8,128)(2,1)} async-done(((bf16[256,4096]{1,0:T(8,128)(2,1)}), bf16[256,2048]{1,0:T(8,128)(2,1)}) %reduce-scatter.8.cloned.1.call-update) | async-done | bytes 1048592 | tf_op jit(solution)/shard_map/reduce_scatter | solution.py:145
  (57 shorter events, 1.2 us)
Async XLA Ops:
  7.2 18.7 %copy-start = (bf16[256,4096]{1,0:T(8,128)(2,1)S(1)}, bf16[256,4096]{1,0:T(8,128)(2,1)}, u32[]{:S(2)}) copy-start(bf16[256,4096]{1,0:T(8,128)(2,1)} %param.7) | copy-start | bytes 6291460
  8.6 38.8 %copy-start.10 = (s32[288]{0:T(512)}, s32[288]{0:T(512)S(1)}, u32[]{:S(2)}) copy-start(s32[288]{0:T(512)S(1)} %fusion.20) | copy-start | bytes 3460
  12.2 21.4 %all-to-all-start = ((s32[16,1,36]{2,1,0:T(1,128)}), s32[16,1,36]{2,1,0:T(1,128)S(1)}, u32[]{:S(2)}, u32[]{:S(2)}) async-start(s32[16,1,36]{2,1,0:T(1,128)} %all_to_all.12), calls=%async_computation | async-start | bytes 16384 | tf_op jit(solution)/shard_map/all_to_all | solution.py:45
  20.6 5.8 %copy-start.1 = (bf16[4096,1024]{1,0:T(8,128)(2,1)S(1)}, bf16[4096,1024]{1,0:T(8,128)(2,1)}, u32[]{:S(2)}) copy-start(bf16[4096,1024]{1,0:T(8,128)(2,1)} %param.8) | copy-start | bytes 25165828
  32.3 1.4 copy-start.7
  33.7 5.5 %copy-start.5 = (pred[16,36]{1,0:T(8,128)(4,1)}, pred[16,36]{1,0:T(8,128)(4,1)S(1)}, u32[]{:S(2)}) copy-start(pred[16,36]{1,0:T(8,128)(4,1)S(1)} %compare_bitcast_fusion) | copy-start | bytes 1732
  33.8 0.6 copy-start.6
  40.4 36.6 %all-to-all-start.1 = ((bf16[16,36,1024]{2,1,0:T(8,128)(2,1)}), bf16[16,36,1024]{2,1,0:T(8,128)(2,1)}, u32[]{:S(2)}, u32[]{:S(2)}) async-start(bf16[16,36,1024]{2,1,0:T(8,128)(2,1)} %broadcast_select_fusion), calls=%async_computation.1 | async-start | bytes 2621440 | tf_op jit(solution)/shard_map/all_to_all | solution.py:50
  47.3 92.9 %all-gather.3.cloned.1.call-start = ((), (), s32[]{:S(2)}) async-start(), calls=%async_computation.10 | async-start | bytes 1114112 | tf_op jit(solution)/shard_map/all_gather | solution.py:57
  82.3 81.6 %copy-start.3 = (bf16[32,9,1024]{2,1,0:T(8,128)(2,1)}, bf16[32,9,1024]{2,1,0:T(8,128)(2,1)S(1)}, u32[]{:S(2)}) copy-start(bf16[32,9,1024]{2,1,0:T(8,128)(2,1)S(1)} %reshape.208) | copy-start | bytes 1769476
  82.3 78.8 %copy-start.11 = (f32[32]{0:T(128)S(1)}, f32[32]{0:T(128)}, u32[]{:S(2)}) copy-start(f32[32]{0:T(128)} %param.11) | copy-start | bytes 388
  83.3 76.4 %all-reduce.4.cloned.1.call-start = ((), (), s32[]{:S(2)}) async-start(), calls=%async_computation.6 | async-start | bytes 131072 | tf_op jit(solution)/shard_map/psum | solution.py:68
  83.3 80.6 %copy-start.14 = (s32[32]{0:T(128)}, s32[32]{0:T(128)S(1)}, u32[]{:S(2)}) copy-start(s32[32]{0:T(128)S(1)} %iota_add_fusion) | copy-start | bytes 388
  83.3 80.6 %copy-start.12 = (f32[32]{0:T(128)}, f32[32]{0:T(128)S(1)}, u32[]{:S(2)}) copy-start(f32[32]{0:T(128)S(1)} %add_rsqrt_fusion.1) | copy-start | bytes 388
  142.5 103.4 %reduce-scatter.6.cloned.1.call-start = ((), (), s32[]{:S(2)}) async-start(), calls=%async_computation.8 | async-start | bytes 2228224 | tf_op jit(solution)/shard_map/reduce_scatter | solution.py:101
  161.2 2.8 copy-start.9
  256.4 24.7 %all-to-all-start.2 = ((bf16[16,36,1024]{2,1,0:T(8,128)(2,1)}), bf16[16,36,1024]{2,1,0:T(8,128)(2,1)S(1)}, u32[]{:S(2)}, u32[]{:S(2)}) async-start(bf16[16,36,1024]{2,1,0:T(8,128)(2,1)} %convert_element_type.53), calls=%async_computation.4 | async-start | bytes 2621440 | tf_op jit(solution)/shard_map/all_to_all | solution.py:120
  260.3 55.8 %reduce-scatter.4.cloned.1.call-start = ((), (), s32[]{:S(2)}) async-start(), calls=%async_computation.7 | async-start | bytes 393216 | tf_op jit(solution)/shard_map/reduce_scatter | solution.py:142
  283.6 14.3 %copy-start.2 = (f32[256,1024]{1,0:T(8,128)S(1)}, f32[256,1024]{1,0:T(8,128)}, u32[]{:S(2)}) copy-start(f32[256,1024]{1,0:T(8,128)} %get-tuple-element.18) | copy-start | bytes 3145732
  283.6 14.3 %copy-start.8 = (f32[256]{0:T(256)S(1)}, f32[256]{0:T(256)}, u32[]{:S(2)}) copy-start(f32[256]{0:T(256)} %copy-done.7) | copy-start | bytes 3076
  286.5 15.3 %copy-start.4 = (f32[32,1024]{1,0:T(8,128)S(1)}, f32[32,1024]{1,0:T(8,128)}, u32[]{:S(2)}) copy-start(f32[32,1024]{1,0:T(8,128)} %get-tuple-element.20) | copy-start | bytes 393220
  286.5 15.3 %copy-start.13 = (f32[32]{0:T(128)S(1)}, f32[32]{0:T(128)}, u32[]{:S(2)}) copy-start(f32[32]{0:T(128)} %copy-done.12) | copy-start | bytes 388
  308.5 20.5 %reduce-scatter.8.cloned.1.call-start = ((), (), s32[]{:S(2)}) async-start(), calls=%async_computation.9 | async-start | bytes 3145728 | tf_op jit(solution)/shard_map/reduce_scatter | solution.py:145
Sparse Core Ops, SparseCore 0:
  83.4 56.7 all-gather.2
  143.1 16.5 all-reduce.3
  164.1 81.7 reduce-scatter.5
  308.6 6.8 reduce-scatter.3
  318.2 10.7 reduce-scatter.7
where the time goes:
time: 337 us; the launch traced here: 336 us
  waiting for transfers between devices  211 us (63%)
  matrix products  32.5 us (10%)
  local copies, waits for them, and re-layouts  26.1 us (8%)
  other arithmetic  24.4 us (7%)
  starting transfers between devices  19.3 us (6%)
  between operations  14.1 us (4%)
  blocking collectives  8.28 us (2%)
    reduce_scatter x1, waiting for transfers between devices, per_device(): lax.psum_scatter(lax.dot_general(sibling_document_slope, search_embedding...  81.7 us
    all_gather x1, waiting for transfers between devices, per_device(): lax.all_gather(matching_document_matrix, 'dp', axis=0, tiled=True)  53 us
    all_to_all x1, waiting for transfers between devices, per_device(): lax.all_to_all(picked_rows, 'dp', split_axis=0, concat_axis=0, tiled=True)  29.6 us
    psum x1, waiting for transfers between devices, per_device(): lax.psum((batch_part, hard_part), 'mp')  16.9 us
    all_to_all x1, waiting for transfers between devices, per_device(): lax.all_to_all(outgoing_grads.reshape(devices, capacity, width).astype(jn...  16.6 us
    reduce_scatter x1, waiting for transfers between devices, per_device(): lax.psum_scatter(p_state.astype(jnp.bfloat16), 'mp', scatter_dimension=1,...  12.9 us
    scatter-add x1, other arithmetic, per_device(): p_grad = jnp.zeros((p_rows, width), jnp.float32).at[jnp.maximum(asked_row...  11.3 us
    all_to_all x1, starting transfers between devices, per_device(): lax.all_to_all(outgoing, 'dp', split_axis=0, concat_axis=0, tiled=True)  8.31 us
  transfers between devices with their start and end apart: 8, of which 6 were waited for; matrix products, arithmetic and copies ran while one was open for 7% of the time, Pallas kernels for 0%

commit v1 on v0

v1 whole, which is shorter than its diff:
```python
import jax
import jax.numpy as jnp
from jax import lax
from jax.sharding import PartitionSpec as P

temperature = 0.02
rows_by_rows = (((1,), (1,)), ((), ()))
first_by_first = (((0,), (0,)), ((), ()))


def per_device(
    query_states, passage_states, head_weight, positives, negatives, search_cost_incoming_slope
):
    q_rows = query_states.shape[0]
    p_rows = passage_states.shape[0]
    half = head_weight.shape[0] // 2
    position = lax.axis_index("dp")
    core = lax.axis_index("mp")
    swap = [(0, 1), (1, 0)]

    lists = jnp.concatenate(
        [
            positives[:, None].astype(jnp.float32),
            negatives.astype(jnp.float32),
            search_cost_incoming_slope[:, None],
        ],
        axis=1,
    )
    all_lists = lax.all_gather(lists, "dp", axis=0, tiled=True)

    q_proj = jnp.dot(query_states, head_weight, preferred_element_type=jnp.float32)
    q_half = lax.all_gather(q_proj.astype(jnp.bfloat16), "dp", axis=0, tiled=True)
    p_proj = jnp.dot(passage_states, head_weight, preferred_element_type=jnp.float32)
    p_half = p_proj.astype(jnp.bfloat16)
    p_square = jnp.sum(p_proj * p_proj, axis=1)
    q_square = jnp.sum(jnp.square(q_half.astype(jnp.float32)), axis=1)
    raw = lax.dot_general(q_half, p_half, rows_by_rows, preferred_element_type=jnp.float32)
    raw, p_square, q_square = [
        x + lax.ppermute(x, "mp", swap) for x in (raw, p_square, q_square)
    ]
    p_inv = lax.rsqrt(p_square + 1e-06)
    q_inv = lax.rsqrt(q_square + 1e-06)
    scores = raw * (q_inv[:, None] * (1.0 / temperature)) * p_inv[None, :]

    numbers = (position * p_rows + jnp.arange(p_rows)).astype(jnp.float32)
    own = (all_lists[:, :1] == numbers[None, :]).astype(jnp.float32)
    weight = jnp.sum(own, axis=0)[None, :]
    for k in range(negatives.shape[1]):
        weight = weight + (all_lists[:, k + 1 : k + 2] == numbers[None, :]).astype(jnp.float32)
    powers = weight * jnp.exp(scores)
    sums = jnp.stack(
        [
            jnp.sum(powers, axis=1),
            jnp.sum(powers * scores, axis=1),
            jnp.sum(own * scores, axis=1),
        ]
    )
    total, moment, hit = lax.psum(sums, "dp")
    slope = all_lists[:, -1]
    grads = (slope * (1.0 / temperature))[:, None] * (
        powers * (1.0 / total)[:, None] - own
    )

    q_part = jnp.dot(
        (grads * p_inv[None, :]).astype(jnp.bfloat16), p_half, preferred_element_type=jnp.float32
    )
    q_grad = lax.psum_scatter(q_part, "dp", scatter_dimension=0, tiled=True)

    p_grad = lax.dot_general(
        (grads * q_inv[:, None]).astype(jnp.bfloat16),
        q_half,
        first_by_first,
        preferred_element_type=jnp.float32,
    )
    p_radial = temperature * jnp.sum(grads * scores, axis=0)
    p_dir = p_inv[:, None] * (p_grad - p_proj * (p_inv * p_radial)[:, None])

    mine = lambda x: lax.dynamic_slice_in_dim(x, position * q_rows, q_rows, 0)
    total, moment, hit, slope, q_inv = [mine(x) for x in (total, moment, hit, slope, q_inv)]
    losses = jnp.log(total) - hit
    q_radial = slope * (moment / total - hit)
    q_dir = q_inv[:, None] * (q_grad - q_proj * (q_inv * q_radial)[:, None])

    near = lax.dynamic_slice_in_dim(head_weight, core * half, half, 0)
    far = lax.dynamic_slice_in_dim(head_weight, (1 - core) * half, half, 0)

    def back(rows):
        rows = rows.astype(jnp.bfloat16)
        sent = lax.dot_general(rows, far, rows_by_rows, preferred_element_type=jnp.float32)
        got = lax.ppermute(sent.astype(jnp.bfloat16), "mp", swap)
        kept = lax.dot_general(rows, near, rows_by_rows, preferred_element_type=jnp.float32)
        return (kept + got.astype(jnp.float32)).astype(jnp.bfloat16)

    return losses, back(q_dir), back(p_dir)


def solution(mesh):
    placed = (P("dp", None), P("dp", None), P(None, "mp"), P("dp"), P("dp", None), P("dp"))
    return jax.shard_map(
        per_device,
        mesh=mesh,
        in_specs=placed,
        out_specs=(P("dp"), P("dp", "mp"), P("dp", "mp")),
        check_vma=False,
    )
```

time: 337 us -> 218 us (0.65)
  waiting for transfers between devices: 211 us -> 76.5 us
  blocking collectives: 8.28 us -> 83.3 us
  local copies, waits for them, and re-layouts: 26.1 us -> 0.94 us
  other arithmetic: 24.4 us -> 4.95 us
  starting transfers between devices: 19.3 us -> 1.26 us
  matrix products: 32.5 us -> 36.4 us
    all_to_all x3 -> x0, waiting for transfers between devices: 46.1 us -> none  [the longest x1 29.6 us: per_device(): lax.all_to_all(picked_rows, 'dp', split_axis=0, concat_axis=0, tiled=True)]
    all_gather x1, waiting for transfers between devices: 53 us -> 8.48 us  [per_device(): lax.all_gather(q_proj.astype(jnp.bfloat16), 'dp', axis=0, tiled=True)]
    all_gather x0 -> x1, blocking collectives: none -> 43 us  [per_device(): all_lists = lax.all_gather(lists, 'dp', axis=0, tiled=True)]
    psum x3 -> x1, blocking collectives: 8.28 us -> 40.3 us  [per_device(): total, moment, hit = lax.psum(sums, 'dp')]
    reduce_scatter x3 -> x1, waiting for transfers between devices: 94.7 us -> 67.2 us  [per_device(): q_grad = lax.psum_scatter(q_part, 'dp', scatter_dimension=0, tiled=True)]
    all_to_all x3 -> x0, starting transfers between devices: 19.1 us -> none  [the longest x1 8.31 us: per_device(): lax.all_to_all(outgoing, 'dp', split_axis=0, concat_axis=0, tiled=True)]
    psum x1 -> x0, waiting for transfers between devices: 16.9 us -> none  [per_device(): lax.psum((batch_part, hard_part), 'mp')]
    scatter-add x1 -> x0, other arithmetic: 11.3 us -> none  [per_device(): p_grad = jnp.zeros((p_rows, width), jnp.float32).at[jnp.maximum(asked_row...]
  transfers between devices with their start and end apart: 8 -> 7, of which waited for: 6 -> 3; matrix products, arithmetic and copies ran while one was open for 7% -> 12% of each run, Pallas kernels for 0% -> 0%
where the time goes in v1:
time: 218 us
  blocking collectives  83.3 us (38%)
  waiting for transfers between devices  76.5 us (35%)
  matrix products  36.4 us (17%)
  between operations  14.2 us (7%)
  other arithmetic  4.95 us (2%)
    reduce_scatter x1, waiting for transfers between devices, per_device(): q_grad = lax.psum_scatter(q_part, 'dp', scatter_dimension=0, tiled=True)  67.2 us
    all_gather x1, blocking collectives, per_device(): all_lists = lax.all_gather(lists, 'dp', axis=0, tiled=True)  43 us
    psum x1, blocking collectives, per_device(): total, moment, hit = lax.psum(sums, 'dp')  40.3 us
    dot_general x2, matrix products, back(): lax.dot_general(rows, near, rows_by_rows, preferred_element_type=jnp.floa...  8.94 us
    all_gather x1, waiting for transfers between devices, per_device(): lax.all_gather(q_proj.astype(jnp.bfloat16), 'dp', axis=0, tiled=True)  8.48 us
    dot_general x2, matrix products, back(): lax.dot_general(rows, far, rows_by_rows, preferred_element_type=jnp.float32)  7.96 us
    dot_general x1, matrix products, per_device(): jnp.dot(passage_states, head_weight, preferred_element_type=jnp.float32)  5.8 us
    dot_general x1, matrix products, per_device(): jnp.dot(query_states, head_weight, preferred_element_type=jnp.float32)  5.78 us
  transfers between devices with their start and end apart: 7, of which 3 were waited for; matrix products, arithmetic and copies ran while one was open for 12% of the time, Pallas kernels for 0%

profile of v1, /device:TPU:0, one launch (start us, length us, event | category | flops | bytes accessed | tf_op | source)
XLA Modules:
  0.0 217.6 jit_solution(4996364443953655201)
XLA Ops:
  7.2 0.0 copy-start
  7.2 0.0 all-gather.3.cloned.1.call-start
  7.2 5.8 %fusion.45 = (bf16[32,1024]{1,0:T(8,128)(2,1)}, f32[32,1024]{1,0:T(8,128)S(1)}) fusion(bf16[32,4096]{1,0:T(8,128)(2,1)} %param.6, bf16[4096,1024]{1,0:T(8,128)(2,1)} %param.8), kind=kOutput, calls=%fused_computation.68 | convolution fusion | flops 268468224 | bytes 8847360 | tf_op jit(solution)/shard_map/dot_general | solution.py:31
  13.0 0.0 all-gather.3.cloned.1.call-update
  13.0 0.0 copy-start.2
  13.0 0.0 copy-start.4
  13.1 0.0 copy-start.3
  13.1 0.0 reduce-scatter.2.cloned.1.call-start
  13.1 0.0 copy-done
  13.1 5.8 %multiply_reduce_fusion.1 = (f32[256]{0:T(256)S(1)}, f32[256,1024]{1,0:T(8,128)S(1)}) fusion(bf16[256,4096]{1,0:T(8,128)(2,1)S(1)} %copy-done, bf16[4096,1024]{1,0:T(8,128)(2,1)} %param.8), kind=kOutput, calls=%fused_computation.14 | convolution fusion | flops 2148007680 | bytes 11535360 | tf_op jit(solution)/shard_map/dot_general | solution.py:33
  18.9 0.0 copy-start.1
  18.9 0.5 collective-permute-start.2
  19.4 0.0 copy-done.2
  19.5 0.0 copy-done.4
  19.5 0.0 copy-done.3
  19.5 43.0 %all-gather = f32[16,32,10]{1,2,0:T(8,128)S(1)} all-gather(f32[1,32,10]{1,2,0:T(8,128)S(1)} %maximum_bitcast_fusion), channel_id=1, replica_groups=mesh['dp'=16,'mp'=2] {'dp'}, dimensions={0}, use_global_device_ids=true | all-gather | bytes 21760 | tf_op jit(solution)/shard_map/all_gather | solution.py:29
  62.5 0.1 reshape.37
  62.7 0.2 convert_reduce_fusion
  62.9 8.5 %all-gather.3.cloned.1.call-done = bf16[512,1024]{1,0:T(8,128)(2,1)} async-done(((bf16[32,1024]{1,0:T(8,128)(2,1)}), bf16[512,1024]{1,0:T(8,128)(2,1)}) %all-gather.3.cloned.1.call-update) | async-done | bytes 1048592 | tf_op jit(solution)/shard_map/all_gather | solution.py:32
  71.4 1.7 fusion.24
  73.1 0.1 collective-permute-start
  73.1 1.5 multiply_reduce_fusion
  74.6 0.6 collective-permute-start.1
  75.2 0.0 collective-permute-done.2
  75.2 0.8 collective-permute-done.1
  76.0 0.0 collective-permute-done
  76.0 0.0 copy-done.1
  76.0 0.7 fusion.42
  76.8 40.3 %psum.7 = f32[3,512]{1,0:T(4,128)S(1)} all-reduce(f32[3,512]{1,0:T(4,128)S(1)} %pad_maximum_fusion), channel_id=1, replica_groups=mesh['dp'=16,'mp'=2] {'dp'}, use_global_device_ids=true, to_apply=%region_6.0 | all-reduce | flops 1536 | bytes 12288 | tf_op jit(solution)/shard_map/psum | solution.py:58
  117.1 3.6 %fusion.16 = f32[512,1024]{1,0:T(8,128)} fusion(f32[512]{0:T(512)S(1)} %bitcast.78, f32[512]{0:T(512)S(1)} %bitcast.81, f32[256]{0:T(256)S(1)} %add_rsqrt_fusion.1, f32[256,1024]{1,0:T(8,128)} %copy-done.1, f32[512]{0:T(512)S(1)} %bitcast.43, f32[256]{0:T(256)S(1)} %add_convert_fusion.2, f32[512,256]{0,1:T(8,128)S(1)} %get-tuple-element.8, ...), kind=kOutput, calls=%fused_computation.26 | convolution fusion | flops 272891904 | bytes 3695616 | tf_op jit(solution)/shard_map/dot_general | solution.py:64
  120.7 0.0 reduce-scatter.2.cloned.1.call-update
  120.7 0.8 multiply_reduce_fusion.2
  121.6 2.6 %multiply_convert_fusion = bf16[256,1024]{1,0:T(8,128)(2,1)S(1)} fusion(f32[256]{0:T(256)S(1)} %add_rsqrt_fusion.1, f32[256,1024]{1,0:T(8,128)} %copy-done.1, f32[256]{0:T(256)S(1)} %multiply_multiply_fusion.1, bf16[512,1024]{1,0:T(8,128)(2,1)} %all-gather.3.cloned.1.call-done, f32[512]{0:T(512)S(1)} %get-tuple-element.10, f32[512]{0:T(512)S(1)} %bitcast.80, ...), kind=kOutput, calls=%fused_computation.13 | convolution fusion | flops 273678336 | bytes 3174400 | tf_op jit(solution)/shard_map/dot_general | solution.py:69
  124.2 0.0 copy-start.5
  124.2 0.8 copy-done.5
  124.9 4.4 %fusion.8 = bf16[256,2048]{1,0:T(8,128)(2,1)} fusion(bf16[256,1024]{1,0:T(8,128)(2,1)S(1)} %multiply_convert_fusion, bf16[4096,1024]{1,0:T(8,128)(2,1)} %param.8, s32[]{:T(128)S(6)} %select_n.15), kind=kOutput, calls=%fused_computation.8 | convolution fusion | flops 1074266112 | bytes 5767172 | tf_op jit(solution)/shard_map/dot_general | solution.py:89
  129.4 0.0 collective-permute-start.4
  129.4 0.6 subtract_bitcast_fusion
  130.0 0.1 fusion.40
  130.1 67.2 %reduce-scatter.2.cloned.1.call-done = f32[32,1024]{1,0:T(8,128)} async-done(((f32[512,1024]{1,0:T(8,128)}), f32[32,1024]{1,0:T(8,128)}) %reduce-scatter.2.cloned.1.call-update) | async-done | bytes 131088 | tf_op jit(solution)/shard_map/reduce_scatter | solution.py:67
  197.3 1.0 multiply_convert_fusion.7
  198.3 3.5 %fusion.11 = bf16[32,2048]{1,0:T(8,128)(2,1)S(1)} fusion(bf16[32,1024]{1,0:T(8,128)(2,1)S(1)} %multiply_convert_fusion.7, bf16[4096,1024]{1,0:T(8,128)(2,1)} %param.8, s32[]{:T(128)S(6)} %select_n.15), kind=kOutput, calls=%fused_computation.9 | convolution fusion | flops 134283264 | bytes 4390916 | tf_op jit(solution)/shard_map/dot_general | solution.py:89
  201.8 0.0 collective-permute-start.3
  201.8 0.0 collective-permute-done.4
  201.8 0.0 copy-done.6
  201.8 4.8 %add_convert_fusion = bf16[256,2048]{1,0:T(8,128)(2,1)} fusion(bf16[256,2048]{1,0:T(8,128)(2,1)} %collective-permute-done.4, bf16[256,1024]{1,0:T(8,128)(2,1)S(1)} %copy-done.6, bf16[4096,1024]{1,0:T(8,128)(2,1)} %param.8, s32[]{:T(128)S(6)} %select_n.14), kind=kOutput, calls=%fused_computation.10 | convolution fusion | flops 1075314688 | bytes 6815748 | tf_op jit(solution)/shard_map/dot_general | solution.py:91
  206.6 0.0 collective-permute-done.3
  206.6 4.2 %add_convert_fusion.1 = bf16[32,2048]{1,0:T(8,128)(2,1)} fusion(bf16[32,2048]{1,0:T(8,128)(2,1)S(1)} %collective-permute-done.3, bf16[32,1024]{1,0:T(8,128)(2,1)S(1)} %multiply_convert_fusion.7, bf16[4096,1024]{1,0:T(8,128)(2,1)} %param.8, s32[]{:T(128)S(6)} %select_n.14), kind=kOutput, calls=%fused_computation.28 | convolution fusion | flops 134414336 | bytes 4521988 | tf_op jit(solution)/shard_map/dot_general | solution.py:91
  (12 shorter events, 0.1 us)
Async XLA Ops:
  7.2 6.0 %copy-start = (bf16[256,4096]{1,0:T(8,128)(2,1)S(1)}, bf16[256,4096]{1,0:T(8,128)(2,1)}, u32[]{:S(2)}) copy-start(bf16[256,4096]{1,0:T(8,128)(2,1)} %param.7) | copy-start | bytes 6291460
  7.2 64.2 %all-gather.3.cloned.1.call-start = ((), (), s32[]{:S(2)}) async-start(), calls=%async_computation.1 | async-start | bytes 1114112 | tf_op jit(solution)/shard_map/all_gather | solution.py:32
  13.0 6.4 %copy-start.2 = (s32[32,8]{0,1:T(8,128)S(1)}, s32[32,8]{0,1:T(8,128)}, u32[]{:S(2)}) copy-start(s32[32,8]{0,1:T(8,128)} %param.10) | copy-start | bytes 3076
  13.0 6.4 %copy-start.4 = (s32[32]{0:T(128)S(1)}, s32[32]{0:T(128)}, u32[]{:S(2)}) copy-start(s32[32]{0:T(128)} %param.9) | copy-start | bytes 388
  13.1 6.4 %copy-start.3 = (f32[32]{0:T(128)S(1)}, f32[32]{0:T(128)}, u32[]{:S(2)}) copy-start(f32[32]{0:T(128)} %param.11) | copy-start | bytes 388
  13.1 184.2 %reduce-scatter.2.cloned.1.call-start = ((), (), s32[]{:S(2)}) async-start(), calls=%async_computation.2 | async-start | bytes 2228224 | tf_op jit(solution)/shard_map/reduce_scatter | solution.py:67
  18.9 57.1 %copy-start.1 = (f32[256,1024]{1,0:T(8,128)}, f32[256,1024]{1,0:T(8,128)S(1)}, u32[]{:S(2)}) copy-start(f32[256,1024]{1,0:T(8,128)S(1)} %get-tuple-element.27) | copy-start | bytes 3145732
  18.9 56.3 %collective-permute-start.2 = (f32[256]{0:T(256)S(1)}, f32[256]{0:T(256)S(1)}, u32[]{:S(2)}, u32[]{:S(2)}) collective-permute-start(f32[256]{0:T(256)S(1)} %get-tuple-element.26), channel_id=1, source_target_pairs={{0,1},{1,0},{2,3},{3,2},{4,5},{5,4},{6,7},{7,6},{8,9},{9,8},{10,11... | collective-permute-start | bytes 3080 | tf_op jit(solution)/shard_map/ppermute | solution.py:39
  73.1 3.0 %collective-permute-start = (f32[512,256]{0,1:T(8,128)S(1)}, f32[512,256]{0,1:T(8,128)S(1)}, u32[]{:S(2)}, u32[]{:S(2)}) collective-permute-start(f32[512,256]{0,1:T(8,128)S(1)} %fusion.24), channel_id=1, source_target_pairs={{0,1},{1,0},{2,3},{3,2},{4,5},{5,4},{6,7},{7,6},{8,9},{9,8},{10,11... | collective-permute-start | bytes 1572872 | tf_op jit(solution)/shard_map/ppermute | solution.py:39
  74.6 1.4 collective-permute-start.1
  124.2 0.8 copy-start.5
  129.4 72.4 %copy-start.6 = (bf16[256,1024]{1,0:T(8,128)(2,1)S(1)}, bf16[256,1024]{1,0:T(8,128)(2,1)}, u32[]{:S(2)}) copy-start(bf16[256,1024]{1,0:T(8,128)(2,1)} %copy-done.5) | copy-start | bytes 1572868
  129.4 72.4 %collective-permute-start.4 = (bf16[256,2048]{1,0:T(8,128)(2,1)}, bf16[256,2048]{1,0:T(8,128)(2,1)}, u32[]{:S(2)}, u32[]{:S(2)}) collective-permute-start(bf16[256,2048]{1,0:T(8,128)(2,1)} %fusion.8), channel_id=1, source_target_pairs={{0,1},{1,0},{2,3},{3,2},{4,5},{5,4},{6,7},{7,6},{8,9},{9,8},{10,11... | collective-permute-start | bytes 3145736 | tf_op jit(solution)/shard_map/ppermute | solution.py:90
  201.8 4.8 %collective-permute-start.3 = (bf16[32,2048]{1,0:T(8,128)(2,1)S(1)}, bf16[32,2048]{1,0:T(8,128)(2,1)S(1)}, u32[]{:S(2)}, u32[]{:S(2)}) collective-permute-start(bf16[32,2048]{1,0:T(8,128)(2,1)S(1)} %fusion.11), channel_id=1, source_target_pairs={{0,1},{1,0},{2,3},{3,2},{4,5},{5,4},{6,7},{7,6},{8,9},{9,8},{10,11... | collective-permute-start | bytes 393224 | tf_op jit(solution)/shard_map/ppermute | solution.py:90
Sparse Core Ops, SparseCore 0:
  13.1 58.1 all-gather.2
  120.9 76.3 reduce-scatter.1

commit v2 on v1

v2 whole, which is shorter than its diff:
```python
import functools

import jax
import jax.numpy as jnp
from jax import lax
from jax.experimental import pallas as pl
from jax.experimental.pallas import tpu as pltpu
from jax.sharding import PartitionSpec as P

temperature = 0.02
by_rows = (((1,), (1,)), ((), ()))
by_first = (((0,), (0,)), ((), ()))
f32 = jnp.float32
bf16 = jnp.bfloat16
tile = 128
w_parts = 8
strip = 32


def dot(x, y, dims=(((1,), (0,)), ((), ()))):
    return lax.dot_general(x, y, dims, preferred_element_type=f32)


def remote(src, dst, send, recv, where):
    return pltpu.make_async_remote_copy(
        src_ref=src,
        dst_ref=dst,
        send_sem=send,
        recv_sem=recv,
        device_id=where,
        device_id_type=pl.DeviceIdType.MESH,
    )


def kernel(
    n,
    names,
    q_hbm,
    p_hbm,
    w_hbm,
    lists_ref,
    loss_ref,
    q_out,
    p_out,
    qs,
    ps,
    w,
    q_proj,
    q_all,
    p_proj,
    p_half,
    p_dir,
    slots,
    lists,
    psq,
    psq_far,
    col,
    raw,
    raw_far,
    g_q,
    g_p,
    t_slots,
    mh,
    mh_slots,
    turn,
    part,
    r1,
    r2,
    r3,
    q_grad,
    p_send,
    p_recv,
    q_send,
    q_recv,
    load,
    pair,
    z_sem,
    x_sem,
    y_sem,
    fx_sem,
    fy_sem,
    list_sem,
    t_sem,
    mh_sem,
    s1_sem,
    s2_sem,
    s3_sem,
    back_sem,
):
    rows, depth = qs.shape
    p_rows, width = p_proj.shape
    queries = q_all.shape[0]
    piece = rows // 2
    group = tile // rows
    na = n // group
    half = depth // 2
    me = lax.axis_index("dp")
    core = lax.axis_index("mp")
    a, b = me // group, lax.rem(me, group)
    x, y = lax.rem(me, 2), lax.rem(me // 2, 2)
    dx, dy = 1 - 2 * x, 2 - 4 * y
    xp, yp, other = {"dp": me + dx}, {"dp": me + dy}, {"mp": 1 - core}

    k_rows = depth // w_parts

    def w_load(i):
        at = pl.ds(pl.multiple_of(i * k_rows, k_rows), k_rows)
        return pltpu.make_async_copy(w_hbm.at[at, :], w.at[at, :], load.at[i])

    q_load = pltpu.make_async_copy(q_hbm, qs, load.at[w_parts])
    p_load = pltpu.make_async_copy(p_hbm, ps, load.at[w_parts + 1])
    q_load.start()
    for i in range(w_parts):
        w_load(i).start()
    p_load.start()

    barrier = pltpu.get_barrier_semaphore()

    @pl.loop(1, n)
    def _(k):
        pl.semaphore_signal(
            barrier,
            inc=1,
            device_id={"dp": lax.rem(me + k, n)},
            device_id_type=pl.DeviceIdType.MESH,
        )

    pl.semaphore_signal(
        barrier, inc=1, device_id=other, device_id_type=pl.DeviceIdType.MESH
    )

    q_load.wait()
    q_proj[...] = jnp.zeros_like(q_proj)

    @pl.loop(0, w_parts)
    def _(i):
        w_load(i).wait()
        at = pl.ds(pl.multiple_of(i * k_rows, k_rows), k_rows)
        q_proj[...] += dot(qs[:, at], w[at, :])

    def block(i):
        return q_all.at[pl.ds(pl.multiple_of(i * rows, rows), rows), :]

    def bit(ref, i, h):
        return ref.at[pl.ds(pl.multiple_of(i * rows + h * piece, piece), piece), :]

    q_all[pl.ds(pl.multiple_of(me * rows, rows), rows), :] = q_proj[...].astype(bf16)
    pl.semaphore_wait(barrier, n)

    def z_copy(s, i):
        to = {"dp": lax.rem(a + s, na) * group + b}
        return remote(block(i), block(i), z_sem.at[0, s], z_sem.at[1, s], to)

    def column(s):
        return lax.rem(a - s + na, na) * group + b

    def x_copy(s, i):
        return remote(block(i), block(i), x_sem.at[0, s], x_sem.at[1, s], xp)

    def y_copy(s, i):
        return remote(block(i), block(i), y_sem.at[0, s], y_sem.at[1, s], yp)

    def fx_copy(s, i):
        return remote(bit(q_all, i, 1), bit(q_all, i, 1), fx_sem.at[0, s], fx_sem.at[1, s], xp)

    def fy_copy(s, i):
        return remote(bit(q_all, i, 0), bit(q_all, i, 0), fy_sem.at[0, s], fy_sem.at[1, s], yp)

    @pl.loop(1, na)
    def _(s):
        z_copy(s, me).start()

    x_copy(0, me).start()
    y_copy(0, me).start()

    q_square = jnp.sum(q_proj[...] * q_proj[...], axis=1, keepdims=True)
    square_rows = jnp.broadcast_to(q_square, (rows, tile))
    square_lanes = jnp.concatenate([square_rows] * group, axis=0).T
    lane = lax.broadcasted_iota(jnp.int32, (16, tile), 1)
    sub = lax.broadcasted_iota(jnp.int32, (16, tile), 0)
    own_list = jnp.where(sub == 10, square_lanes[0:16, :], lists_ref[...])
    slots[me] = jnp.where(lane // rows == b, own_list, 0.0)

    def list_copy(k, i):
        to = {"dp": lax.rem(me + k, n)}
        return remote(slots.at[i], slots.at[i], list_sem.at[0, k], list_sem.at[1, k], to)

    def before(k):
        return lax.rem(me - k + n, n)

    @pl.loop(1, n)
    def _(k):
        list_copy(k, me).start()

    p_load.wait()
    p_chunk = 256
    p_steps = width // p_chunk
    psq[...] = jnp.zeros_like(psq)
    for j in range(p_steps):
        at = slice(j * p_chunk, (j + 1) * p_chunk)
        out = dot(ps[...], w[:, at])
        p_proj[:, at] = out
        p_half[:, at] = out.astype(bf16)
        psq[...] += jnp.broadcast_to(jnp.sum(out * out, axis=1, keepdims=True), psq.shape)
        lo = 1 + j * (na - 1) // p_steps
        hi = 1 + (j + 1) * (na - 1) // p_steps

        @pl.loop(lo, hi)
        def _(s):
            z_copy(s, column(s)).wait_recv()
            x_copy(s, column(s)).start()
            y_copy(s, column(s)).start()

    psq_copy = remote(psq, psq_far, pair.at[0], pair.at[1], other)
    psq_copy.start()

    @pl.loop(0, na)
    def _(s):
        x_copy(s, column(s) + dx).wait_recv()
        fy_copy(s, column(s) + dx).start()
        y_copy(s, column(s) + dy).wait_recv()
        fx_copy(s, column(s) + dy).start()

    @pl.loop(1, n)
    def _(k):
        list_copy(k, before(k)).wait_recv()

    @pl.loop(0, na)
    def _(t):
        full = slots[t * group]
        for g in range(1, group):
            full = full + slots[t * group + g]
        lists[:, pl.ds(pl.multiple_of(t * tile, tile), tile)] = full

    def strip_of(i):
        return pl.ds(pl.multiple_of(i * strip, strip), strip)

    def numbers_of(i):
        first = me * p_rows + i * strip
        return (first + lax.broadcasted_iota(jnp.int32, (strip, 1), 0)).astype(f32)

    def is_own(i):
        return (lists[0:1, :] == numbers_of(i)).astype(f32)

    @pl.loop(0, p_rows // strip)
    def _(i):
        numbers = numbers_of(i)
        named = jnp.sum(is_own(i), axis=1, keepdims=True)
        col[strip_of(i), :] = jnp.broadcast_to(named, (strip, tile))
        times = (lists[1:2, :] == numbers).astype(f32)
        for k in range(2, names):
            times = times + (lists[k : k + 1, :] == numbers).astype(f32)
        g_q[strip_of(i), :] = times.astype(bf16)

    raw[p_rows : p_rows + 8, :] = jnp.broadcast_to(lists[10:11, :], (8, queries))
    psq_copy.wait_recv()

    @pl.loop(0, na)
    def _(s):
        fx_copy(s, column(s) + dx + dy).wait_recv()
        fy_copy(s, column(s) + dx + dy).wait_recv()

    s_chunk = 256

    @pl.loop(0, queries // s_chunk)
    def _(i):
        at = pl.ds(pl.multiple_of(i * s_chunk, s_chunk), s_chunk)
        raw[0:p_rows, at] = dot(p_half[...], q_all[at, :], by_rows)

    raw_copy = remote(raw, raw_far, pair.at[2], pair.at[3], other)
    raw_copy.start()
    raw_copy.wait()

    def q_scale():
        return lax.rsqrt(raw[p_rows : p_rows + 1, :] + raw_far[p_rows : p_rows + 1, :] + 1e-06)

    def p_scale(at):
        return lax.rsqrt(psq[at, 0:1] + psq_far[at, 0:1] + 1e-06)

    zero = jnp.zeros((1, queries), f32)

    def score_strip(i, sums):
        at = strip_of(i)
        scores = (raw[at, :] + raw_far[at, :]) * (q_scale() * (1.0 / temperature)) * p_scale(at)
        powers = (col[at, 0:1] + g_q[at, :].astype(f32)) * jnp.exp(scores)
        raw[at, :] = scores
        raw_far[at, :] = powers
        new = (powers, powers * scores, is_own(i) * scores)
        return tuple(s + jnp.sum(v, axis=0, keepdims=True) for s, v in zip(sums, new))

    total, moment, hit = lax.fori_loop(0, p_rows // strip, score_strip, (zero, zero, zero))

    t_slots[me] = total
    for t in range(na):
        at = slice(t * tile, (t + 1) * tile)
        mh[t] = jnp.concatenate([moment[:, at], hit[:, at], jnp.zeros((6, tile), f32)], axis=0)
    mh_slots[me] = mh[a]

    def t_copy(k, i):
        to = {"dp": lax.rem(me + k, n)}
        return remote(t_slots.at[i], t_slots.at[i], t_sem.at[0, k], t_sem.at[1, k], to)

    def mh_copy(k, i):
        peer = lax.rem(me + k, n)
        return remote(
            mh.at[peer // group], mh_slots.at[i], mh_sem.at[0, k], mh_sem.at[1, k], {"dp": peer}
        )

    @pl.loop(1, n)
    def _(k):
        t_copy(k, me).start()

    @pl.loop(1, n)
    def _(k):
        mh_copy(k, me).start()

    @pl.loop(1, n)
    def _(k):
        t_copy(k, before(k)).wait_recv()

    total = lax.fori_loop(0, n, lambda i, s: s + t_slots[i], zero)

    @pl.loop(0, p_rows // strip)
    def _(i):
        at = strip_of(i)
        slope = lists[9:10, :] * (1.0 / temperature)
        grads = slope * (raw_far[at, :] * (1.0 / total) - is_own(i))
        g_q[at, :] = (grads * p_scale(at)).astype(bf16)
        g_p[at, :] = (grads * q_scale()).astype(bf16)
        radial = temperature * jnp.sum(grads * raw[at, :], axis=1, keepdims=True)
        col[at, :] = jnp.broadcast_to(radial, (strip, tile))

    def owner(s):
        return lax.rem(a + s, na) * group + b

    def s1_copy(s, h, c):
        i = owner(s) + (dx if h else dy) + (dx + dy - (dx if h else dy)) * c
        return remote(
            bit(part, i, h),
            r1.at[s, h, c],
            s1_sem.at[0, s, 2 * h + c],
            s1_sem.at[1, s, 2 * h + c],
            xp if h else yp,
        )

    def s2_copy(s, h):
        i = owner(s) + (dy if h else dx)
        return remote(
            bit(part, i, h), r2.at[s, h], s2_sem.at[0, s, h], s2_sem.at[1, s, h], yp if h else xp
        )

    def s3_copy(s):
        i = owner(s)
        src = part.at[pl.ds(pl.multiple_of(i * rows, rows), rows), :]
        return remote(src, r3.at[s], s3_sem.at[0, s], s3_sem.at[1, s], {"dp": i})

    @pl.loop(0, na)
    def _(j):
        s = lax.rem(j + 1, na)
        at = pl.ds(pl.multiple_of(lax.rem(a + s, na) * tile, tile), tile)
        part[at, :] = dot(g_q[:, at], p_half[...], by_first).astype(bf16)
        for c in (1, 0):
            for h in range(2):
                s1_copy(s, h, c).start()

    for j in range(p_steps):
        at = slice(j * p_chunk, (j + 1) * p_chunk)
        grad = dot(g_p[...], q_all[:, at])
        inv = p_scale(slice(0, p_rows))
        p_dir[:, at] = (inv * (grad - p_proj[:, at] * (inv * col[:, 0:1]))).astype(bf16)

    @pl.loop(0, na)
    def _(j):
        s = lax.rem(j + 1, na)
        for h in range(2):
            s1_copy(s, h, 1).wait_recv()
            ref = bit(part, owner(s) + (dy if h else dx), h)
            ref[...] = (ref[...].astype(f32) + r1[s, h, 1].astype(f32)).astype(bf16)
            s2_copy(s, h).start()

    out_chunk = p_send.shape[2]
    out_steps = half // out_chunk

    def back_rows(which, c):
        return pl.ds(pl.multiple_of(which * half + c * out_chunk, out_chunk), out_chunk)

    def p_copy(c):
        return remote(p_send.at[c], p_recv.at[c], back_sem.at[0, c], back_sem.at[1, c], other)

    @pl.loop(0, out_steps)
    def _(c):
        p_send[c] = dot(p_dir[...], w[back_rows(1 - core, c), :], by_rows).astype(bf16)
        p_copy(c).start()

    def first_sum(s, h):
        s1_copy(s, h, 0).wait_recv()
        s2_copy(s, h).wait_recv()
        mine = bit(part, owner(s), h)[...].astype(f32)
        return mine + r1[s, h, 0].astype(f32) + r2[s, h].astype(f32)

    @pl.loop(1, na)
    def _(s):
        for h in range(2):
            bit(part, owner(s), h)[...] = first_sum(s, h).astype(bf16)
        s3_copy(s).start()

    for h in range(2):
        q_grad[h * piece : (h + 1) * piece, :] = first_sum(0, h)

    @pl.loop(0, out_steps)
    def _(c):
        kept = dot(p_dir[...], w[back_rows(core, c), :], by_rows)
        p_copy(c).wait_recv()
        at = pl.ds(pl.multiple_of(c * out_chunk, out_chunk), out_chunk)
        p_out[:, at] = (kept + p_recv[c].astype(f32)).astype(bf16)

    @pl.loop(1, n)
    def _(k):
        mh_copy(k, before(k)).wait_recv()

    sums = lax.fori_loop(0, n, lambda i, s: s + mh_slots[i], jnp.zeros((8, tile), f32))
    at = pl.ds(pl.multiple_of(a * tile, tile), tile)
    t_own = lax.fori_loop(
        0, n, lambda i, s: s + t_slots[i, :, at], jnp.zeros((1, tile), f32)
    )
    inv = lax.rsqrt(raw[p_rows : p_rows + 1, at] + raw_far[p_rows : p_rows + 1, at] + 1e-06)
    own_moment, own_hit = sums[0:1, :], sums[1:2, :]
    loss = jnp.log(t_own) - own_hit
    radial = lists[9:10, at] * (own_moment / t_own - own_hit)
    three = jnp.concatenate([loss, inv, inv * radial, jnp.zeros((5, tile), f32)], axis=0)
    turn[...] = jnp.concatenate([three] * (tile // 8), axis=0).T
    mine = turn[pl.ds(pl.multiple_of(b * rows, rows), rows), :]
    loss_ref[...] = mine

    @pl.loop(1, na)
    def _(s):
        s3_copy(s).wait_recv()
        q_grad[...] += r3[s].astype(f32)

    q_dir = (mine[:, 1:2] * (q_grad[...] - q_proj[...] * mine[:, 2:3])).astype(bf16)
    qs[:, 0:width] = q_dir

    q_copy = remote(q_send, q_recv, pair.at[4], pair.at[5], other)

    @pl.loop(0, out_steps)
    def _(c):
        to = pl.ds(pl.multiple_of(c * out_chunk, out_chunk), out_chunk)
        q_send[:, to] = dot(qs[:, 0:width], w[back_rows(1 - core, c), :], by_rows).astype(bf16)

    q_copy.start()

    @pl.loop(0, out_steps)
    def _(c):
        to = pl.ds(pl.multiple_of(c * out_chunk, out_chunk), out_chunk)
        q_grad[:, 0:out_chunk] = dot(qs[:, 0:width], w[back_rows(core, c), :], by_rows)
        q_out[:, to] = q_grad[:, 0:out_chunk].astype(bf16)

    q_copy.wait_recv()
    q_out[...] = (q_out[...].astype(f32) + q_recv[...].astype(f32)).astype(bf16)

    q_copy.wait_send()
    psq_copy.wait_send()

    @pl.loop(0, out_steps)
    def _(c):
        p_copy(c).wait_send()

    @pl.loop(1, n)
    def _(k):
        list_copy(k, me).wait_send()
        t_copy(k, me).wait_send()
        mh_copy(k, me).wait_send()

    @pl.loop(0, na)
    def _(s):
        x_copy(s, column(s)).wait_send()
        y_copy(s, column(s)).wait_send()
        fy_copy(s, column(s) + dx).wait_send()
        fx_copy(s, column(s) + dy).wait_send()
        for h in range(2):
            s1_copy(s, h, 0).wait_send()
            s1_copy(s, h, 1).wait_send()
            s2_copy(s, h).wait_send()

    @pl.loop(1, na)
    def _(s):
        z_copy(s, me).wait_send()
        s3_copy(s).wait_send()


def per_device(
    n, query_states, passage_states, head_weight, positives, negatives, search_cost_incoming_slope
):
    rows, depth = query_states.shape
    p_rows = passage_states.shape[0]
    width = head_weight.shape[1]
    half = depth // 2
    queries = n * rows
    group = tile // rows
    na = n // group
    piece = rows // 2
    names = 1 + negatives.shape[1]
    steps = 4
    lists = jnp.concatenate(
        [
            positives[None, :].astype(f32),
            negatives.T.astype(f32),
            search_cost_incoming_slope[None, :],
            jnp.zeros((16 - names - 1, rows), f32),
        ],
        axis=0,
    )
    lists = jnp.concatenate([lists] * group, axis=1)
    dma = pltpu.SemaphoreType.DMA
    vmem = pltpu.VMEM
    flops = 2 * width * (2 * (rows + p_rows) * depth + 3 * queries * p_rows)
    out = pl.pallas_call(
        functools.partial(kernel, n, names),
        out_shape=(
            jax.ShapeDtypeStruct((rows, tile), f32),
            jax.ShapeDtypeStruct((rows, half), bf16),
            jax.ShapeDtypeStruct((p_rows, half), bf16),
        ),
        in_specs=[pl.BlockSpec(memory_space=pl.ANY)] * 3
        + [pl.BlockSpec(memory_space=pltpu.VMEM)],
        out_specs=[pl.BlockSpec(memory_space=pltpu.VMEM)] * 3,
        scratch_shapes=[
            vmem((rows, depth), bf16),
            vmem((p_rows, depth), bf16),
            vmem((depth, width), bf16),
            vmem((rows, width), f32),
            vmem((queries, width), bf16),
            vmem((p_rows, width), f32),
            vmem((p_rows, width), bf16),
            vmem((p_rows, width), bf16),
            vmem((n, 16, tile), f32),
            vmem((16, queries), f32),
            vmem((p_rows, tile), f32),
            vmem((p_rows, tile), f32),
            vmem((p_rows, tile), f32),
            vmem((p_rows + 8, queries), f32),
            vmem((p_rows + 8, queries), f32),
            vmem((p_rows, queries), bf16),
            vmem((p_rows, queries), bf16),
            vmem((n, 1, queries), f32),
            vmem((na, 8, tile), f32),
            vmem((n, 8, tile), f32),
            vmem((tile, tile), f32),
            vmem((queries, width), bf16),
            vmem((na, 2, 2, piece, width), bf16),
            vmem((na, 2, piece, width), bf16),
            vmem((na, rows, width), bf16),
            vmem((rows, width), f32),
            vmem((steps, p_rows, half // steps), bf16),
            vmem((steps, p_rows, half // steps), bf16),
            vmem((rows, half), bf16),
            vmem((rows, half), bf16),
            dma((w_parts + 2,)),
            dma((6,)),
            dma((2, na)),
            dma((2, na)),
            dma((2, na)),
            dma((2, na)),
            dma((2, na)),
            dma((2, n)),
            dma((2, n)),
            dma((2, n)),
            dma((2, na, 4)),
            dma((2, na, 2)),
            dma((2, na)),
            dma((2, steps)),
        ],
        compiler_params=pltpu.CompilerParams(
            collective_id=0, has_side_effects=True, vmem_limit_bytes=60 * 2**20
        ),
        cost_estimate=pl.CostEstimate(
            flops=flops, bytes_accessed=12 * 2**20, transcendentals=queries * p_rows
        ),
        name="contrastive",
    )(query_states, passage_states, head_weight, lists)
    return out[0][:, 0], out[1], out[2]


def solution(mesh):
    placed = (P("dp", None), P("dp", None), P(None, "mp"), P("dp"), P("dp", None), P("dp"))
    return jax.shard_map(
        functools.partial(per_device, mesh.shape["dp"]),
        mesh=mesh,
        in_specs=placed,
        out_specs=(P("dp"), P("dp", "mp"), P("dp", "mp")),
        check_vma=False,
    )
```

time: 218 us -> 63.9 us (0.29)
  blocking collectives: 83.3 us -> 0 us
  waiting for transfers between devices: 76.5 us -> 0 us
  Pallas kernels: 0 us -> 54.8 us
  matrix products: 36.4 us -> 0 us
  between operations: 14.2 us -> 0.64 us
  local copies, waits for them, and re-layouts: 0.94 us -> 5.21 us
    reduce_scatter x1 -> x0, waiting for transfers between devices: 67.2 us -> none  [per_device(): q_grad = lax.psum_scatter(q_part, 'dp', scatter_dimension=0, tiled=True)]
    pallas_call x0 -> x1, Pallas kernels: none -> 54.8 us  [per_device(): pl.pallas_call(functools.partial(kernel, n, names), out_shape=(jax.ShapeD...]
    all_gather x1 -> x0, blocking collectives: 43 us -> none  [per_device(): all_lists = lax.all_gather(lists, 'dp', axis=0, tiled=True)]
    psum x1 -> x0, blocking collectives: 40.3 us -> none  [per_device(): total, moment, hit = lax.psum(sums, 'dp')]
    dot_general x9 -> x0, matrix products: 36.4 us -> none  [the longest x2 8.94 us: back(): lax.dot_general(rows, near, rows_by_rows, preferred_element_type=jnp.floa...]
    all_gather x1 -> x0, waiting for transfers between devices: 8.48 us -> none  [per_device(): lax.all_gather(q_proj.astype(jnp.bfloat16), 'dp', axis=0, tiled=True)]
    reduce_sum x4 -> x0, other arithmetic: 3.22 us -> none  [the longest x1 1.5 us: per_device(): q_square = jnp.sum(jnp.square(q_half.astype(jnp.float32)), axis=1)]
    unnamed x15 -> x2, local copies, waits for them, and re-layouts: 0.91 us -> 3.87 us
  transfers between devices with their start and end apart: 7 -> 0, of which waited for: 3 -> 0; matrix products, arithmetic and copies ran while one was open for 12% -> 0% of each run, Pallas kernels for 0% -> 0%
where the time goes in v2:
time: 63.9 us; the launch traced here: 63.5 us
  Pallas kernels  54.8 us (86%)
  local copies, waits for them, and re-layouts  5.21 us (8%)
  other arithmetic  2.84 us (4%)
  between operations  0.64 us (1%)
    pallas_call x1, Pallas kernels, per_device(): pl.pallas_call(functools.partial(kernel, n, names), out_shape=(jax.ShapeD...  54.8 us
    unnamed x2, local copies, waits for them, and re-layouts  3.87 us
    concatenate x1, other arithmetic, per_device(): lists = jnp.concatenate([lists] * group, axis=1)  1.49 us
    slice x1, local copies, waits for them, and re-layouts, per_device(): return (out[0][:, 0], out[1], out[2])  1.34 us

profile of v2, /device:TPU:0, one launch (start us, length us, event | category | flops | bytes accessed | tf_op | source)
XLA Modules:
  0.0 63.5 jit_solution(4195364397287980368)
XLA Ops:
  0.6 0.7 %convert_bitcast_fusion.1 = f32[1,32]{1,0:T(1,128)S(1)} fusion(s32[32]{0:T(128)} %param.9), kind=kLoop, calls=%fused_computation.3 | loop fusion | flops 32 | bytes 256 | tf_op jit(solution)/shard_map/convert_element_type | solution.py:506
  1.3 0.7 %convert_bitcast_fusion = f32[8,32]{1,0:T(8,128)S(1)} fusion(s32[32,8]{0,1:T(8,128)} %param.10), kind=kLoop, calls=%fused_computation.2 | loop fusion | flops 256 | bytes 2048 | tf_op jit(solution)/shard_map/convert_element_type | solution.py:507
  2.0 1.5 %maximum_maximum_fusion.lists_ref = f32[16,128]{1,0:T(8,128)} fusion(f32[6,32]{1,0:T(8,128)S(1)} %broadcast_in_dim.8, f32[1,32]{1,0:T(1,128)} %bitcast.5, f32[8,32]{1,0:T(8,128)S(1)} %convert_bitcast_fusion, f32[1,32]{1,0:T(1,128)S(1)} %convert_bitcast_fusion.1), kind=kLoop, calls=%fused_computation.1 | loop fusion | flops 30720 | bytes 10240 | tf_op jit(solution)/shard_map/concatenate | solution.py:513
  3.5 54.8 %contrastive.1 = (f32[32,128]{1,0:T(8,128)}, bf16[32,2048]{1,0:T(8,128)(2,1)}, bf16[256,2048]{1,0:T(8,128)(2,1)}) custom-call(bf16[32,4096]{1,0:T(8,128)(2,1)} %q_hbm.1, bf16[256,4096]{1,0:T(8,128)(2,1)} %p_hbm.1, bf16[4096,1024]{1,0:T(8,128)(2,1)} %w_hbm.1, f32[16,128]{1,0:T(8,128)} %maximum_maximum_fusion.lists_ref), custom_call_target="tpu_custom_call" | custom-call | flops 5637144576 | bytes 12582912 | tf_op jit(solution)/shard_map/contrastive/pallas_call | solution.py:517
  58.3 1.3 %slice_reduce_fusion = f32[32]{0:T(128)} fusion(f32[32,128]{1,0:T(8,128)} %get-tuple-element.6), kind=kLoop, calls=%fused_computation | loop fusion | bytes 256 | tf_op jit(solution)/shard_map/slice | solution.py:581
  59.6 1.6 %copy.11 = bf16[32,2048]{1,0:T(8,128)(2,1)} copy(bf16[32,2048]{1,0:T(8,128)(2,1)} %get-tuple-element.13) | data formatting | bytes 262144
  61.2 2.3 %copy.12 = bf16[256,2048]{1,0:T(8,128)(2,1)} copy(bf16[256,2048]{1,0:T(8,128)(2,1)} %get-tuple-element.14) | data formatting | bytes 2097152
  (1 shorter events, 0.0 us)

commit v3 on v2

--- a/solution.py
+++ b/solution.py
@@ -14,7 +14,9 @@
 bf16 = jnp.bfloat16
 tile = 128
 w_parts = 8
+window = 4
 strip = 32
+s_chunk = 512
 
 
 def dot(x, y, dims=(((1,), (0,)), ((), ()))):
@@ -38,7 +40,9 @@
     q_hbm,
     p_hbm,
     w_hbm,
-    lists_ref,
+    pos_ref,
+    neg_ref,
+    slope_ref,
     loss_ref,
     q_out,
     p_out,
@@ -51,6 +55,7 @@
     p_half,
     p_dir,
     slots,
+    sq_slots,
     lists,
     psq,
     psq_far,
@@ -72,20 +77,25 @@
     p_recv,
     q_send,
     q_recv,
+    p_done,
     load,
     pair,
+    raw_sem,
     z_sem,
     x_sem,
     y_sem,
     fx_sem,
     fy_sem,
     list_sem,
+    sq_sem,
     t_sem,
     mh_sem,
     s1_sem,
     s2_sem,
     s3_sem,
     back_sem,
+    q_sem,
+    done_sem,
 ):
     rows, depth = qs.shape
     p_rows, width = p_proj.shape
@@ -110,9 +120,8 @@
     q_load = pltpu.make_async_copy(q_hbm, qs, load.at[w_parts])
     p_load = pltpu.make_async_copy(p_hbm, ps, load.at[w_parts + 1])
     q_load.start()
-    for i in range(w_parts):
+    for i in range(window):
         w_load(i).start()
-    p_load.start()
 
     barrier = pltpu.get_barrier_semaphore()
 
@@ -129,12 +138,56 @@
         barrier, inc=1, device_id=other, device_id_type=pl.DeviceIdType.MESH
     )
 
+    def before(k):
+        return lax.rem(me - k + n, n)
+
+    def list_copy(k, i):
+        to = {"dp": lax.rem(me + k, n)}
+        return remote(slots.at[i], slots.at[i], list_sem.at[0, k], list_sem.at[1, k], to)
+
+    def sq_copy(k, i):
+        to = {"dp": lax.rem(me + k, n)}
+        return remote(sq_slots.at[i], sq_slots.at[i], sq_sem.at[0, k], sq_sem.at[1, k], to)
+
+    turn[0:24, :] = jnp.zeros((24, tile), f32)
+    turn[0 : names - 1, 0:rows] = neg_ref[...].astype(f32)
+    turn[8:9, 0:rows] = pos_ref[...].astype(f32)
+    turn[16:17, 0:rows] = slope_ref[...]
+    neg_lanes, pos_lanes, slope_lanes = [
+        pltpu.roll(turn[8 * i : 8 * i + 8, :], b * rows, 1) for i in range(3)
+    ]
+    lane = lax.broadcasted_iota(jnp.int32, (1, tile), 1)
+    mask = lane // rows == b
+    slots[me] = jnp.concatenate(
+        [
+            pos_lanes[0:1, :],
+            neg_lanes[0 : names - 1, :],
+            slope_lanes[0:1, :],
+            jnp.zeros((15 - names, tile), f32),
+        ],
+        axis=0,
+    )
+    pl.semaphore_wait(barrier, n)
+
+    @pl.loop(1, n)
+    def _(k):
+        list_copy(k, me).start()
+
     q_load.wait()
     q_proj[...] = jnp.zeros_like(q_proj)
 
     @pl.loop(0, w_parts)
     def _(i):
         w_load(i).wait()
+
+        @pl.when(i < w_parts - window)
+        def _():
+            w_load(i + window).start()
+
+        @pl.when(i == w_parts - window)
+        def _():
+            p_load.start()
+
         at = pl.ds(pl.multiple_of(i * k_rows, k_rows), k_rows)
         q_proj[...] += dot(qs[:, at], w[at, :])
 
@@ -145,8 +198,6 @@
         return ref.at[pl.ds(pl.multiple_of(i * rows + h * piece, piece), piece), :]
 
     q_all[pl.ds(pl.multiple_of(me * rows, rows), rows), :] = q_proj[...].astype(bf16)
-    pl.semaphore_wait(barrier, n)
-
     def z_copy(s, i):
         to = {"dp": lax.rem(a + s, na) * group + b}
         return remote(block(i), block(i), z_sem.at[0, s], z_sem.at[1, s], to)
@@ -176,21 +227,11 @@
     q_square = jnp.sum(q_proj[...] * q_proj[...], axis=1, keepdims=True)
     square_rows = jnp.broadcast_to(q_square, (rows, tile))
     square_lanes = jnp.concatenate([square_rows] * group, axis=0).T
-    lane = lax.broadcasted_iota(jnp.int32, (16, tile), 1)
-    sub = lax.broadcasted_iota(jnp.int32, (16, tile), 0)
-    own_list = jnp.where(sub == 10, square_lanes[0:16, :], lists_ref[...])
-    slots[me] = jnp.where(lane // rows == b, own_list, 0.0)
-
-    def list_copy(k, i):
-        to = {"dp": lax.rem(me + k, n)}
-        return remote(slots.at[i], slots.at[i], list_sem.at[0, k], list_sem.at[1, k], to)
-
-    def before(k):
-        return lax.rem(me - k + n, n)
-
-    @pl.loop(1, n)
-    def _(k):
-        list_copy(k, me).start()
+    sq_slots[me] = jnp.where(mask, square_lanes[0:1, :], 0.0)
+
+    @pl.loop(1, n)
+    def _(k):
+        sq_copy(k, me).start()
 
     p_load.wait()
     p_chunk = 256
@@ -224,13 +265,17 @@
     @pl.loop(1, n)
     def _(k):
         list_copy(k, before(k)).wait_recv()
+        sq_copy(k, before(k)).wait_recv()
 
     @pl.loop(0, na)
     def _(t):
-        full = slots[t * group]
+        at = pl.ds(pl.multiple_of(t * tile, tile), tile)
+        full, square = slots[t * group], sq_slots[t * group]
         for g in range(1, group):
             full = full + slots[t * group + g]
-        lists[:, pl.ds(pl.multiple_of(t * tile, tile), tile)] = full
+            square = square + sq_slots[t * group + g]
+        lists[:, at] = full
+        raw[p_rows : p_rows + 8, at] = jnp.broadcast_to(square, (8, tile))
 
     def strip_of(i):
         return pl.ds(pl.multiple_of(i * strip, strip), strip)
@@ -252,7 +297,6 @@
             times = times + (lists[k : k + 1, :] == numbers).astype(f32)
         g_q[strip_of(i), :] = times.astype(bf16)
 
-    raw[p_rows : p_rows + 8, :] = jnp.broadcast_to(lists[10:11, :], (8, queries))
     psq_copy.wait_recv()
 
     @pl.loop(0, na)
@@ -260,16 +304,24 @@
         fx_copy(s, column(s) + dx + dy).wait_recv()
         fy_copy(s, column(s) + dx + dy).wait_recv()
 
-    s_chunk = 256
-
-    @pl.loop(0, queries // s_chunk)
-    def _(i):
-        at = pl.ds(pl.multiple_of(i * s_chunk, s_chunk), s_chunk)
-        raw[0:p_rows, at] = dot(p_half[...], q_all[at, :], by_rows)
-
-    raw_copy = remote(raw, raw_far, pair.at[2], pair.at[3], other)
-    raw_copy.start()
-    raw_copy.wait()
+    s_rows = p_rows // 2
+    sq_far_copy = remote(
+        raw.at[p_rows : p_rows + 8, :], raw_far.at[p_rows : p_rows + 8, :], pair.at[4], pair.at[5], other
+    )
+    sq_far_copy.start()
+
+    def raw_copy(i):
+        at = pl.ds(pl.multiple_of(i * s_rows, s_rows), s_rows)
+        return remote(raw.at[at, :], raw_far.at[at, :], raw_sem.at[0, i], raw_sem.at[1, i], other)
+
+    for i in range(2):
+        at = slice(i * s_rows, (i + 1) * s_rows)
+        for j in range(queries // s_chunk):
+            to = slice(j * s_chunk, (j + 1) * s_chunk)
+            raw[at, to] = dot(p_half[at, :], q_all[to, :], by_rows)
+        raw_copy(i).start()
+
+    sq_far_copy.wait()
 
     def q_scale():
         return lax.rsqrt(raw[p_rows : p_rows + 1, :] + raw_far[p_rows : p_rows + 1, :] + 1e-06)
@@ -288,7 +340,12 @@
         new = (powers, powers * scores, is_own(i) * scores)
         return tuple(s + jnp.sum(v, axis=0, keepdims=True) for s, v in zip(sums, new))
 
-    total, moment, hit = lax.fori_loop(0, p_rows // strip, score_strip, (zero, zero, zero))
+    sums = (zero, zero, zero)
+    s_strips = s_rows // strip
+    for i in range(2):
+        raw_copy(i).wait()
+        sums = lax.fori_loop(i * s_strips, (i + 1) * s_strips, score_strip, sums)
+    total, moment, hit = sums
 
     t_slots[me] = total
     for t in range(na):
@@ -369,6 +426,25 @@
         inv = p_scale(slice(0, p_rows))
         p_dir[:, at] = (inv * (grad - p_proj[:, at] * (inv * col[:, 0:1]))).astype(bf16)
 
+    out_chunk = p_send.shape[2]
+    out_steps = half // out_chunk
+
+    def back_rows(which, c):
+        return pl.ds(pl.multiple_of(which * half + c * out_chunk, out_chunk), out_chunk)
+
+    def p_copy(c):
+        return remote(p_send.at[c], p_recv.at[c], back_sem.at[0, c], back_sem.at[1, c], other)
+
+    def p_far(c):
+        p_send[c] = dot(p_dir[...], w[back_rows(1 - core, c), :], by_rows).astype(bf16)
+        p_copy(c).start()
+
+    def first_sum(s, h):
+        s1_copy(s, h, 0).wait_recv()
+        s2_copy(s, h).wait_recv()
+        mine = bit(part, owner(s), h)[...].astype(f32)
+        return mine + r1[s, h, 0].astype(f32) + r2[s, h].astype(f32)
+
     @pl.loop(0, na)
     def _(j):
         s = lax.rem(j + 1, na)
@@ -378,41 +454,32 @@
             ref[...] = (ref[...].astype(f32) + r1[s, h, 1].astype(f32)).astype(bf16)
             s2_copy(s, h).start()
 
-    out_chunk = p_send.shape[2]
-    out_steps = half // out_chunk
-
-    def back_rows(which, c):
-        return pl.ds(pl.multiple_of(which * half + c * out_chunk, out_chunk), out_chunk)
-
-    def p_copy(c):
-        return remote(p_send.at[c], p_recv.at[c], back_sem.at[0, c], back_sem.at[1, c], other)
-
-    @pl.loop(0, out_steps)
-    def _(c):
-        p_send[c] = dot(p_dir[...], w[back_rows(1 - core, c), :], by_rows).astype(bf16)
-        p_copy(c).start()
-
-    def first_sum(s, h):
-        s1_copy(s, h, 0).wait_recv()
-        s2_copy(s, h).wait_recv()
-        mine = bit(part, owner(s), h)[...].astype(f32)
-        return mine + r1[s, h, 0].astype(f32) + r2[s, h].astype(f32)
-
-    @pl.loop(1, na)
-    def _(s):
-        for h in range(2):
-            bit(part, owner(s), h)[...] = first_sum(s, h).astype(bf16)
-        s3_copy(s).start()
+        @pl.when(j < out_steps)
+        def _():
+            p_far(j)
+
+        @pl.when(j >= 1)
+        def _():
+            for h in range(2):
+                bit(part, owner(j), h)[...] = first_sum(j, h).astype(bf16)
+            s3_copy(j).start()
+
+    for c in range(na, out_steps):
+        p_far(c)
 
     for h in range(2):
         q_grad[h * piece : (h + 1) * piece, :] = first_sum(0, h)
+
+    def done_copy(c):
+        at = pl.ds(pl.multiple_of(c * out_chunk, out_chunk), out_chunk)
+        return pltpu.make_async_copy(p_done.at[c], p_out.at[:, at], done_sem.at[c])
 
     @pl.loop(0, out_steps)
     def _(c):
         kept = dot(p_dir[...], w[back_rows(core, c), :], by_rows)
         p_copy(c).wait_recv()
-        at = pl.ds(pl.multiple_of(c * out_chunk, out_chunk), out_chunk)
-        p_out[:, at] = (kept + p_recv[c].astype(f32)).astype(bf16)
+        p_done[c] = (kept + p_recv[c].astype(f32)).astype(bf16)
+        done_copy(c).start()
 
     @pl.loop(1, n)
     def _(k):
@@ -430,7 +497,7 @@
     three = jnp.concatenate([loss, inv, inv * radial, jnp.zeros((5, tile), f32)], axis=0)
     turn[...] = jnp.concatenate([three] * (tile // 8), axis=0).T
     mine = turn[pl.ds(pl.multiple_of(b * rows, rows), rows), :]
-    loss_ref[...] = mine
+    loss_ref[...] = pltpu.roll(three, lax.rem(tile - b * rows, tile), 1)[0:1, 0:rows]
 
     @pl.loop(1, na)
     def _(s):
@@ -440,34 +507,33 @@
     q_dir = (mine[:, 1:2] * (q_grad[...] - q_proj[...] * mine[:, 2:3])).astype(bf16)
     qs[:, 0:width] = q_dir
 
-    q_copy = remote(q_send, q_recv, pair.at[4], pair.at[5], other)
+    def q_copy(c):
+        return remote(q_send.at[c], q_recv.at[c], q_sem.at[0, c], q_sem.at[1, c], other)
+
+    @pl.loop(0, out_steps)
+    def _(c):
+        q_send[c] = dot(qs[:, 0:width], w[back_rows(1 - core, c), :], by_rows).astype(bf16)
+        q_copy(c).start()
 
     @pl.loop(0, out_steps)
     def _(c):
         to = pl.ds(pl.multiple_of(c * out_chunk, out_chunk), out_chunk)
-        q_send[:, to] = dot(qs[:, 0:width], w[back_rows(1 - core, c), :], by_rows).astype(bf16)
-
-    q_copy.start()
-
-    @pl.loop(0, out_steps)
-    def _(c):
-        to = pl.ds(pl.multiple_of(c * out_chunk, out_chunk), out_chunk)
-        q_grad[:, 0:out_chunk] = dot(qs[:, 0:width], w[back_rows(core, c), :], by_rows)
-        q_out[:, to] = q_grad[:, 0:out_chunk].astype(bf16)
-
-    q_copy.wait_recv()
-    q_out[...] = (q_out[...].astype(f32) + q_recv[...].astype(f32)).astype(bf16)
-
-    q_copy.wait_send()
+        kept = dot(qs[:, 0:width], w[back_rows(core, c), :], by_rows)
+        q_copy(c).wait_recv()
+        q_out[:, to] = (kept + q_recv[c].astype(f32)).astype(bf16)
+
     psq_copy.wait_send()
 
     @pl.loop(0, out_steps)
     def _(c):
         p_copy(c).wait_send()
+        q_copy(c).wait_send()
+        done_copy(c).wait()
 
     @pl.loop(1, n)
     def _(k):
         list_copy(k, me).wait_send()
+        sq_copy(k, me).wait_send()
         t_copy(k, me).wait_send()
         mh_copy(k, me).wait_send()
 
@@ -486,6 +552,22 @@
     def _(s):
         z_copy(s, me).wait_send()
         s3_copy(s).wait_send()
+
+
+def hand_over(loss, q, p, loss_out, q_out, p_out, sems):
+    parts = sems.shape[0] - 2
+    size = p.shape[0] // parts
+    copies = [
+        pltpu.make_async_copy(loss, loss_out, sems.at[0]),
+        pltpu.make_async_copy(q, q_out, sems.at[1]),
+    ]
+    for i in range(parts):
+        at = slice(i * size, (i + 1) * size)
+        copies.append(pltpu.make_async_copy(p.at[at, :], p_out.at[at, :], sems.at[2 + i]))
+    for copy in copies:
+        copy.start()
+    for copy in copies:
+        copy.wait()
 
 
 def per_device(
@@ -501,29 +583,20 @@
     piece = rows // 2
     names = 1 + negatives.shape[1]
     steps = 4
-    lists = jnp.concatenate(
-        [
-            positives[None, :].astype(f32),
-            negatives.T.astype(f32),
-            search_cost_incoming_slope[None, :],
-            jnp.zeros((16 - names - 1, rows), f32),
-        ],
-        axis=0,
-    )
-    lists = jnp.concatenate([lists] * group, axis=1)
     dma = pltpu.SemaphoreType.DMA
     vmem = pltpu.VMEM
     flops = 2 * width * (2 * (rows + p_rows) * depth + 3 * queries * p_rows)
     out = pl.pallas_call(
         functools.partial(kernel, n, names),
         out_shape=(
-            jax.ShapeDtypeStruct((rows, tile), f32),
+            jax.ShapeDtypeStruct((1, rows), f32),
             jax.ShapeDtypeStruct((rows, half), bf16),
             jax.ShapeDtypeStruct((p_rows, half), bf16),
         ),
         in_specs=[pl.BlockSpec(memory_space=pl.ANY)] * 3
-        + [pl.BlockSpec(memory_space=pltpu.VMEM)],
-        out_specs=[pl.BlockSpec(memory_space=pltpu.VMEM)] * 3,
+        + [pl.BlockSpec(memory_space=pltpu.VMEM)] * 3,
+        out_specs=[pl.BlockSpec(memory_space=pltpu.VMEM)] * 2
+        + [pl.BlockSpec(memory_space=pl.ANY)],
         scratch_shapes=[
             vmem((rows, depth), bf16),
             vmem((p_rows, depth), bf16),
@@ -534,6 +607,7 @@
             vmem((p_rows, width), bf16),
             vmem((p_rows, width), bf16),
             vmem((n, 16, tile), f32),
+            vmem((n, 1, tile), f32),
             vmem((16, queries), f32),
             vmem((p_rows, tile), f32),
             vmem((p_rows, tile), f32),
@@ -553,10 +627,12 @@
             vmem((rows, width), f32),
             vmem((steps, p_rows, half // steps), bf16),
             vmem((steps, p_rows, half // steps), bf16),
-            vmem((rows, half), bf16),
-            vmem((rows, half), bf16),
+            vmem((steps, rows, half // steps), bf16),
+            vmem((steps, rows, half // steps), bf16),
+            vmem((steps, p_rows, half // steps), bf16),
             dma((w_parts + 2,)),
             dma((6,)),
+            dma((2, 2)),
             dma((2, na)),
             dma((2, na)),
             dma((2, na)),
@@ -565,10 +641,13 @@
             dma((2, n)),
             dma((2, n)),
             dma((2, n)),
+            dma((2, n)),
             dma((2, na, 4)),
             dma((2, na, 2)),
             dma((2, na)),
             dma((2, steps)),
+            dma((2, steps)),
+            dma((steps,)),
         ],
         compiler_params=pltpu.CompilerParams(
             collective_id=0, has_side_effects=True, vmem_limit_bytes=60 * 2**20
@@ -577,8 +656,24 @@
             flops=flops, bytes_accessed=12 * 2**20, transcendentals=queries * p_rows
         ),
         name="contrastive",
-    )(query_states, passage_states, head_weight, lists)
-    return out[0][:, 0], out[1], out[2]
+    )(
+        query_states,
+        passage_states,
+        head_weight,
+        positives.reshape(1, rows),
+        negatives.T,
+        search_cost_incoming_slope.reshape(1, rows),
+    )
+    losses, q_rows, p_rows_out = pl.pallas_call(
+        hand_over,
+        out_shape=tuple(jax.ShapeDtypeStruct(x.shape, x.dtype) for x in out),
+        in_specs=[pl.BlockSpec(memory_space=pl.ANY)] * 3,
+        out_specs=[pl.BlockSpec(memory_space=pl.ANY)] * 3,
+        scratch_shapes=[dma((2 + steps,))],
+        compiler_params=pltpu.CompilerParams(vmem_limit_bytes=60 * 2**20),
+        name="hand_over",
+    )(*out)
+    return losses.reshape(rows), q_rows, p_rows_out
 
 
 def solution(mesh):

time: 63.9 us -> 93.6 us (1.46)
  Pallas kernels: 54.8 us -> 92.8 us
  local copies, waits for them, and re-layouts: 5.21 us -> 0 us
  other arithmetic: 2.84 us -> 0 us
    pallas_call x0 -> x1, Pallas kernels: none -> 36.9 us  [per_device(): pl.pallas_call(hand_over, out_shape=tuple((jax.ShapeDtypeStruct(x.shape,...]
    unnamed x2 -> x0, local copies, waits for them, and re-layouts: 3.87 us -> none
    concatenate x1 -> x0, other arithmetic: 1.49 us -> none  [per_device(): lists = jnp.concatenate([lists] * group, axis=1)]
    convert_element_type x2 -> x0, other arithmetic: 1.35 us -> none  [the longest x1 0.69 us: per_device(): negatives.T.astype(f32)]
    slice x1 -> x0, local copies, waits for them, and re-layouts: 1.34 us -> none  [per_device(): return (out[0][:, 0], out[1], out[2])]
    pallas_call x1, Pallas kernels: 54.8 us -> 55.9 us  [per_device(): pl.pallas_call(functools.partial(kernel, n, names), out_shape=(jax.ShapeD...]
where the time goes in v3:
time: 93.6 us; the launch traced here: 93.4 us
  Pallas kernels  92.8 us (99%)
    pallas_call x1, Pallas kernels, per_device(): pl.pallas_call(functools.partial(kernel, n, names), out_shape=(jax.ShapeD...  55.9 us
    pallas_call x1, Pallas kernels, per_device(): pl.pallas_call(hand_over, out_shape=tuple((jax.ShapeDtypeStruct(x.shape,...  36.9 us

profile of v3, /device:TPU:0, one launch (start us, length us, event | category | flops | bytes accessed | tf_op | source)
XLA Modules:
  0.0 93.4 jit_solution(17736272379424504701)
XLA Ops:
  0.6 55.9 %contrastive.1 = (f32[1,32]{1,0:T(1,128)}, bf16[32,2048]{1,0:T(8,128)(2,1)}, bf16[256,2048]{1,0:T(8,128)(2,1)}) custom-call(bf16[32,4096]{1,0:T(8,128)(2,1)} %q_hbm.1, bf16[256,4096]{1,0:T(8,128)(2,1)} %p_hbm.1, bf16[4096,1024]{1,0:T(8,128)(2,1)} %w_hbm.1, s32[1,32]{1,0:T(1,128)} %bitcast.5, s32[8,32]{1,0:T(8,128)} %bitcast.4, f32[1,32]{1,0:T(1,128)} %bitcast.6), custom_call_target="tpu_custom_call" | custom-call | flops 5637144576 | bytes 12582912 | tf_op jit(solution)/shard_map/contrastive/pallas_call | solution.py:589
  56.5 36.9 %hand_over.1 = (f32[1,32]{1,0:T(1,128)}, bf16[32,2048]{1,0:T(8,128)(2,1)}, bf16[256,2048]{1,0:T(8,128)(2,1)}) custom-call(f32[1,32]{1,0:T(1,128)} %get-tuple-element.9.loss, bf16[32,2048]{1,0:T(8,128)(2,1)} %get-tuple-element.10.q, bf16[256,2048]{1,0:T(8,128)(2,1)} %get-tuple-element.11.p), custom_call_target="tpu_custom_call" | custom-call | tf_op jit(solution)/shard_map/hand_over/pallas_call | solution.py:667

commit v4 on v3

--- a/solution.py
+++ b/solution.py
@@ -369,10 +369,6 @@
 
     @pl.loop(1, n)
     def _(k):
-        mh_copy(k, me).start()
-
-    @pl.loop(1, n)
-    def _(k):
         t_copy(k, before(k)).wait_recv()
 
     total = lax.fori_loop(0, n, lambda i, s: s + t_slots[i], zero)
@@ -419,6 +415,10 @@
         for c in (1, 0):
             for h in range(2):
                 s1_copy(s, h, c).start()
+
+    @pl.loop(1, n)
+    def _(k):
+        mh_copy(k, me).start()
 
     for j in range(p_steps):
         at = slice(j * p_chunk, (j + 1) * p_chunk)
@@ -554,20 +554,23 @@
         s3_copy(s).wait_send()
 
 
-def hand_over(loss, q, p, loss_out, q_out, p_out, sems):
-    parts = sems.shape[0] - 2
+def hand_over(loss, q, p, loss_out, q_out, p_out, loss_buf, q_buf, p_buf, sems):
+    parts = sems.shape[1] - 2
     size = p.shape[0] // parts
-    copies = [
-        pltpu.make_async_copy(loss, loss_out, sems.at[0]),
-        pltpu.make_async_copy(q, q_out, sems.at[1]),
-    ]
+    routes = [(loss, loss_buf, loss_out), (q, q_buf, q_out)]
     for i in range(parts):
         at = slice(i * size, (i + 1) * size)
-        copies.append(pltpu.make_async_copy(p.at[at, :], p_out.at[at, :], sems.at[2 + i]))
-    for copy in copies:
-        copy.start()
-    for copy in copies:
-        copy.wait()
+        routes.append((p.at[at, :], p_buf.at[at, :], p_out.at[at, :]))
+    into = [pltpu.make_async_copy(x, y, sems.at[0, i]) for i, (x, y, _) in enumerate(routes)]
+    away = [pltpu.make_async_copy(y, z, sems.at[1, i]) for i, (_, y, z) in enumerate(routes)]
+    order = list(range(2, parts + 2)) + [0, 1]
+    for i in order:
+        into[i].start()
+    for i in order:
+        into[i].wait()
+        away[i].start()
+    for i in order:
+        away[i].wait()
 
 
 def per_device(
@@ -669,7 +672,7 @@
         out_shape=tuple(jax.ShapeDtypeStruct(x.shape, x.dtype) for x in out),
         in_specs=[pl.BlockSpec(memory_space=pl.ANY)] * 3,
         out_specs=[pl.BlockSpec(memory_space=pl.ANY)] * 3,
-        scratch_shapes=[dma((2 + steps,))],
+        scratch_shapes=[vmem(x.shape, x.dtype) for x in out] + [dma((2, 2 + steps))],
         compiler_params=pltpu.CompilerParams(vmem_limit_bytes=60 * 2**20),
         name="hand_over",
     )(*out)

time: 93.6 us -> 59.5 us (0.64)
  Pallas kernels: 92.8 us -> 58.7 us
    pallas_call x1, Pallas kernels: 36.9 us -> 2.06 us  [per_device(): pl.pallas_call(hand_over, out_shape=tuple((jax.ShapeDtypeStruct(x.shape,...]
where the time goes in v4:
time: 59.5 us; the launch traced here: 59.3 us
  Pallas kernels  58.7 us (99%)
  between operations  0.64 us (1%)
    pallas_call x1, Pallas kernels, per_device(): pl.pallas_call(functools.partial(kernel, n, names), out_shape=(jax.ShapeD...  56.6 us
    pallas_call x1, Pallas kernels, per_device(): pl.pallas_call(hand_over, out_shape=tuple((jax.ShapeDtypeStruct(x.shape,...  2.06 us

profile of v4, /device:TPU:0, one launch (start us, length us, event | category | flops | bytes accessed | tf_op | source)
XLA Modules:
  0.0 59.3 jit_solution(9186915440464331044)
XLA Ops:
  0.6 56.6 %contrastive.1 = (f32[1,32]{1,0:T(1,128)}, bf16[32,2048]{1,0:T(8,128)(2,1)}, bf16[256,2048]{1,0:T(8,128)(2,1)}) custom-call(bf16[32,4096]{1,0:T(8,128)(2,1)} %q_hbm.1, bf16[256,4096]{1,0:T(8,128)(2,1)} %p_hbm.1, bf16[4096,1024]{1,0:T(8,128)(2,1)} %w_hbm.1, s32[1,32]{1,0:T(1,128)} %bitcast.5, s32[8,32]{1,0:T(8,128)} %bitcast.4, f32[1,32]{1,0:T(1,128)} %bitcast.6), custom_call_target="tpu_custom_call" | custom-call | flops 5637144576 | bytes 12582912 | tf_op jit(solution)/shard_map/contrastive/pallas_call | solution.py:592
  57.2 2.1 %hand_over.1 = (f32[1,32]{1,0:T(1,128)}, bf16[32,2048]{1,0:T(8,128)(2,1)}, bf16[256,2048]{1,0:T(8,128)(2,1)}) custom-call(f32[1,32]{1,0:T(1,128)} %get-tuple-element.9.loss, bf16[32,2048]{1,0:T(8,128)(2,1)} %get-tuple-element.10.q, bf16[256,2048]{1,0:T(8,128)(2,1)} %get-tuple-element.11.p), custom_call_target="tpu_custom_call" | custom-call | tf_op jit(solution)/shard_map/hand_over/pallas_call | solution.py:670

commit v5 on v4

--- a/solution.py
+++ b/solution.py
@@ -174,22 +174,17 @@
         list_copy(k, me).start()
 
     q_load.wait()
-    q_proj[...] = jnp.zeros_like(q_proj)
-
-    @pl.loop(0, w_parts)
-    def _(i):
+    total = None
+    for i in range(w_parts):
         w_load(i).wait()
-
-        @pl.when(i < w_parts - window)
-        def _():
+        if i + window < w_parts:
             w_load(i + window).start()
-
-        @pl.when(i == w_parts - window)
-        def _():
+        if i + window == w_parts:
             p_load.start()
-
-        at = pl.ds(pl.multiple_of(i * k_rows, k_rows), k_rows)
-        q_proj[...] += dot(qs[:, at], w[at, :])
+        at = slice(i * k_rows, (i + 1) * k_rows)
+        term = dot(qs[:, at], w[at, :])
+        total = term if total is None else total + term
+    q_proj[...] = total
 
     def block(i):
         return q_all.at[pl.ds(pl.multiple_of(i * rows, rows), rows), :]
@@ -505,29 +500,32 @@
         q_grad[...] += r3[s].astype(f32)
 
     q_dir = (mine[:, 1:2] * (q_grad[...] - q_proj[...] * mine[:, 2:3])).astype(bf16)
-    qs[:, 0:width] = q_dir
 
     def q_copy(c):
         return remote(q_send.at[c], q_recv.at[c], q_sem.at[0, c], q_sem.at[1, c], other)
 
-    @pl.loop(0, out_steps)
-    def _(c):
-        q_send[c] = dot(qs[:, 0:width], w[back_rows(1 - core, c), :], by_rows).astype(bf16)
+    q_chunk = q_send.shape[2]
+    q_steps = half // q_chunk
+
+    def q_back(which, c):
+        at = pl.ds(pl.multiple_of(which * half + c * q_chunk, q_chunk), q_chunk)
+        return dot(q_dir, w[at, :], by_rows)
+
+    for c in range(q_steps):
+        q_send[c] = q_back(1 - core, c).astype(bf16)
         q_copy(c).start()
-
-    @pl.loop(0, out_steps)
-    def _(c):
-        to = pl.ds(pl.multiple_of(c * out_chunk, out_chunk), out_chunk)
-        kept = dot(qs[:, 0:width], w[back_rows(core, c), :], by_rows)
+    for c in range(q_steps):
+        kept = q_back(core, c)
         q_copy(c).wait_recv()
-        q_out[:, to] = (kept + q_recv[c].astype(f32)).astype(bf16)
+        q_out[:, c * q_chunk : (c + 1) * q_chunk] = (kept + q_recv[c].astype(f32)).astype(bf16)
 
     psq_copy.wait_send()
+    for c in range(q_steps):
+        q_copy(c).wait_send()
 
     @pl.loop(0, out_steps)
     def _(c):
         p_copy(c).wait_send()
-        q_copy(c).wait_send()
         done_copy(c).wait()
 
     @pl.loop(1, n)
@@ -630,8 +628,8 @@
             vmem((rows, width), f32),
             vmem((steps, p_rows, half // steps), bf16),
             vmem((steps, p_rows, half // steps), bf16),
-            vmem((steps, rows, half // steps), bf16),
-            vmem((steps, rows, half // steps), bf16),
+            vmem((2, rows, half // 2), bf16),
+            vmem((2, rows, half // 2), bf16),
             vmem((steps, p_rows, half // steps), bf16),
             dma((w_parts + 2,)),
             dma((6,)),
@@ -649,11 +647,11 @@
             dma((2, na, 2)),
             dma((2, na)),
             dma((2, steps)),
-            dma((2, steps)),
+            dma((2, 2)),
             dma((steps,)),
         ],
         compiler_params=pltpu.CompilerParams(
-            collective_id=0, has_side_effects=True, vmem_limit_bytes=60 * 2**20
+            collective_id=0, has_side_effects=True, vmem_limit_bytes=63 * 2**20
         ),
         cost_estimate=pl.CostEstimate(
             flops=flops, bytes_accessed=12 * 2**20, transcendentals=queries * p_rows

time: 59.5 us -> 58.8 us (0.988)
  Pallas kernels: 58.7 us -> 58 us
    pallas_call x1, Pallas kernels: 56.6 us -> 55.9 us  [per_device(): pl.pallas_call(functools.partial(kernel, n, names), out_shape=(jax.ShapeD...]
where the time goes in v5:
time: 58.8 us; the launch traced here: 58.6 us
  Pallas kernels  58 us (99%)
  between operations  0.64 us (1%)
    pallas_call x1, Pallas kernels, per_device(): pl.pallas_call(functools.partial(kernel, n, names), out_shape=(jax.ShapeD...  55.9 us
    pallas_call x1, Pallas kernels, per_device(): pl.pallas_call(hand_over, out_shape=tuple((jax.ShapeDtypeStruct(x.shape,...  2.06 us

profile of v5, /device:TPU:0, one launch (start us, length us, event | category | flops | bytes accessed | tf_op | source)
XLA Modules:
  0.0 58.6 jit_solution(9467223443708671831)
XLA Ops:
  0.6 55.9 %contrastive.1 = (f32[1,32]{1,0:T(1,128)}, bf16[32,2048]{1,0:T(8,128)(2,1)}, bf16[256,2048]{1,0:T(8,128)(2,1)}) custom-call(bf16[32,4096]{1,0:T(8,128)(2,1)} %q_hbm.1, bf16[256,4096]{1,0:T(8,128)(2,1)} %p_hbm.1, bf16[4096,1024]{1,0:T(8,128)(2,1)} %w_hbm.1, s32[1,32]{1,0:T(1,128)} %bitcast.5, s32[8,32]{1,0:T(8,128)} %bitcast.4, f32[1,32]{1,0:T(1,128)} %bitcast.6), custom_call_target="tpu_custom_call" | custom-call | flops 5637144576 | bytes 12582912 | tf_op jit(solution)/shard_map/contrastive/pallas_call | solution.py:590
  56.6 2.1 %hand_over.1 = (f32[1,32]{1,0:T(1,128)}, bf16[32,2048]{1,0:T(8,128)(2,1)}, bf16[256,2048]{1,0:T(8,128)(2,1)}) custom-call(f32[1,32]{1,0:T(1,128)} %get-tuple-element.9.loss, bf16[32,2048]{1,0:T(8,128)(2,1)} %get-tuple-element.10.q, bf16[256,2048]{1,0:T(8,128)(2,1)} %get-tuple-element.11.p), custom_call_target="tpu_custom_call" | custom-call | tf_op jit(solution)/shard_map/hand_over/pallas_call | solution.py:668

commit v6 on v5

--- a/solution.py
+++ b/solution.py
@@ -82,10 +82,8 @@
     pair,
     raw_sem,
     z_sem,
-    x_sem,
-    y_sem,
-    fx_sem,
-    fy_sem,
+    first_sem,
+    then_sem,
     list_sem,
     sq_sem,
     t_sem,
@@ -99,7 +97,7 @@
 ):
     rows, depth = qs.shape
     p_rows, width = p_proj.shape
-    queries = q_all.shape[0]
+    queries, wide = q_all.shape[1:]
     piece = rows // 2
     group = tile // rows
     na = n // group
@@ -111,11 +109,13 @@
     dx, dy = 1 - 2 * x, 2 - 4 * y
     xp, yp, other = {"dp": me + dx}, {"dp": me + dy}, {"mp": 1 - core}
 
-    k_rows = depth // w_parts
+    k_parts = w_parts // 2
+    k_rows = depth // k_parts
 
     def w_load(i):
-        at = pl.ds(pl.multiple_of(i * k_rows, k_rows), k_rows)
-        return pltpu.make_async_copy(w_hbm.at[at, :], w.at[at, :], load.at[i])
+        at = slice(i % k_parts * k_rows, (i % k_parts + 1) * k_rows)
+        to = slice(i // k_parts * wide, (i // k_parts + 1) * wide)
+        return pltpu.make_async_copy(w_hbm.at[at, to], w.at[at, to], load.at[i])
 
     q_load = pltpu.make_async_copy(q_hbm, qs, load.at[w_parts])
     p_load = pltpu.make_async_copy(p_hbm, ps, load.at[w_parts + 1])
@@ -173,51 +173,55 @@
     def _(k):
         list_copy(k, me).start()
 
-    q_load.wait()
-    total = None
-    for i in range(w_parts):
-        w_load(i).wait()
-        if i + window < w_parts:
-            w_load(i + window).start()
-        if i + window == w_parts:
-            p_load.start()
-        at = slice(i * k_rows, (i + 1) * k_rows)
-        term = dot(qs[:, at], w[at, :])
-        total = term if total is None else total + term
-    q_proj[...] = total
-
-    def block(i):
-        return q_all.at[pl.ds(pl.multiple_of(i * rows, rows), rows), :]
-
-    def bit(ref, i, h):
-        return ref.at[pl.ds(pl.multiple_of(i * rows + h * piece, piece), piece), :]
-
-    q_all[pl.ds(pl.multiple_of(me * rows, rows), rows), :] = q_proj[...].astype(bf16)
-    def z_copy(s, i):
-        to = {"dp": lax.rem(a + s, na) * group + b}
-        return remote(block(i), block(i), z_sem.at[0, s], z_sem.at[1, s], to)
+    hop = ((xp, dx), (yp, dy))
+
+    def block(h, i):
+        return q_all.at[h, pl.ds(pl.multiple_of(i * rows, rows), rows), :]
 
     def column(s):
         return lax.rem(a - s + na, na) * group + b
 
-    def x_copy(s, i):
-        return remote(block(i), block(i), x_sem.at[0, s], x_sem.at[1, s], xp)
-
-    def y_copy(s, i):
-        return remote(block(i), block(i), y_sem.at[0, s], y_sem.at[1, s], yp)
-
-    def fx_copy(s, i):
-        return remote(bit(q_all, i, 1), bit(q_all, i, 1), fx_sem.at[0, s], fx_sem.at[1, s], xp)
-
-    def fy_copy(s, i):
-        return remote(bit(q_all, i, 0), bit(q_all, i, 0), fy_sem.at[0, s], fy_sem.at[1, s], yp)
-
-    @pl.loop(1, na)
-    def _(s):
-        z_copy(s, me).start()
-
-    x_copy(0, me).start()
-    y_copy(0, me).start()
+    def z_copy(h, s, i):
+        to = {"dp": lax.rem(a + s, na) * group + b}
+        return remote(block(h, i), block(h, i), z_sem.at[0, h, s], z_sem.at[1, h, s], to)
+
+    def first_copy(h, s, i):
+        return remote(
+            block(h, i), block(h, i), first_sem.at[0, h, s], first_sem.at[1, h, s], hop[h][0]
+        )
+
+    def then_copy(h, s, c, i):
+        return remote(
+            block(h, i), block(h, i), then_sem.at[0, h, s, c], then_sem.at[1, h, s, c], hop[1 - h][0]
+        )
+
+    def hand_on(s):
+        for h in range(2):
+            i = column(s) + hop[h][1]
+            first_copy(h, s, i).wait_recv()
+            then_copy(h, s, 1, i).start()
+
+    q_load.wait()
+    for h in range(2):
+        total = None
+        for i in range(h * k_parts, (h + 1) * k_parts):
+            w_load(i).wait()
+            if i + window < w_parts:
+                w_load(i + window).start()
+            if i + window == w_parts:
+                p_load.start()
+            at = slice(i % k_parts * k_rows, (i % k_parts + 1) * k_rows)
+            term = dot(qs[:, at], w[at, h * wide : (h + 1) * wide])
+            total = term if total is None else total + term
+        q_proj[:, h * wide : (h + 1) * wide] = total
+        q_all[h, pl.ds(pl.multiple_of(me * rows, rows), rows), :] = total.astype(bf16)
+        first_copy(h, 0, me).start()
+
+        @pl.loop(1, na)
+        def _(s):
+            z_copy(h, s, me).start()
+
+        then_copy(h, 0, 0, me).start()
 
     q_square = jnp.sum(q_proj[...] * q_proj[...], axis=1, keepdims=True)
     square_rows = jnp.broadcast_to(q_square, (rows, tile))
@@ -238,24 +242,21 @@
         p_proj[:, at] = out
         p_half[:, at] = out.astype(bf16)
         psq[...] += jnp.broadcast_to(jnp.sum(out * out, axis=1, keepdims=True), psq.shape)
-        lo = 1 + j * (na - 1) // p_steps
-        hi = 1 + (j + 1) * (na - 1) // p_steps
+        lo = 1 + -(-j * (na - 1) // p_steps)
+        hi = 1 + -(-(j + 1) * (na - 1) // p_steps)
 
         @pl.loop(lo, hi)
         def _(s):
-            z_copy(s, column(s)).wait_recv()
-            x_copy(s, column(s)).start()
-            y_copy(s, column(s)).start()
+            hand_on(s - 1)
+            for h in range(2):
+                z_copy(h, s, column(s)).wait_recv()
+                first_copy(h, s, column(s)).start()
+                then_copy(h, s, 0, column(s)).start()
 
     psq_copy = remote(psq, psq_far, pair.at[0], pair.at[1], other)
     psq_copy.start()
 
-    @pl.loop(0, na)
-    def _(s):
-        x_copy(s, column(s) + dx).wait_recv()
-        fy_copy(s, column(s) + dx).start()
-        y_copy(s, column(s) + dy).wait_recv()
-        fx_copy(s, column(s) + dy).start()
+    hand_on(na - 1)
 
     @pl.loop(1, n)
     def _(k):
@@ -296,8 +297,9 @@
 
     @pl.loop(0, na)
     def _(s):
-        fx_copy(s, column(s) + dx + dy).wait_recv()
-        fy_copy(s, column(s) + dx + dy).wait_recv()
+        for h in range(2):
+            then_copy(h, s, 0, column(s) + hop[1 - h][1]).wait_recv()
+            then_copy(h, s, 1, column(s) + dx + dy).wait_recv()
 
     s_rows = p_rows // 2
     sq_far_copy = remote(
@@ -313,7 +315,9 @@
         at = slice(i * s_rows, (i + 1) * s_rows)
         for j in range(queries // s_chunk):
             to = slice(j * s_chunk, (j + 1) * s_chunk)
-            raw[at, to] = dot(p_half[at, :], q_all[to, :], by_rows)
+            raw[at, to] = dot(p_half[at, 0:wide], q_all[0, to, :], by_rows) + dot(
+                p_half[at, wide:], q_all[1, to, :], by_rows
+            )
         raw_copy(i).start()
 
     sq_far_copy.wait()
@@ -378,6 +382,9 @@
         radial = temperature * jnp.sum(grads * raw[at, :], axis=1, keepdims=True)
         col[at, :] = jnp.broadcast_to(radial, (strip, tile))
 
+    def bit(ref, i, h):
+        return ref.at[pl.ds(pl.multiple_of(i * rows + h * piece, piece), piece), :]
+
     def owner(s):
         return lax.rem(a + s, na) * group + b
 
@@ -417,7 +424,8 @@
 
     for j in range(p_steps):
         at = slice(j * p_chunk, (j + 1) * p_chunk)
-        grad = dot(g_p[...], q_all[:, at])
+        h = j * p_chunk // wide
+        grad = dot(g_p[...], q_all[h, :, j * p_chunk - h * wide : (j + 1) * p_chunk - h * wide])
         inv = p_scale(slice(0, p_rows))
         p_dir[:, at] = (inv * (grad - p_proj[:, at] * (inv * col[:, 0:1]))).astype(bf16)
 
@@ -537,18 +545,18 @@
 
     @pl.loop(0, na)
     def _(s):
-        x_copy(s, column(s)).wait_send()
-        y_copy(s, column(s)).wait_send()
-        fy_copy(s, column(s) + dx).wait_send()
-        fx_copy(s, column(s) + dy).wait_send()
         for h in range(2):
+            first_copy(h, s, column(s)).wait_send()
+            then_copy(h, s, 0, column(s)).wait_send()
+            then_copy(h, s, 1, column(s) + hop[h][1]).wait_send()
             s1_copy(s, h, 0).wait_send()
             s1_copy(s, h, 1).wait_send()
             s2_copy(s, h).wait_send()
 
     @pl.loop(1, na)
     def _(s):
-        z_copy(s, me).wait_send()
+        for h in range(2):
+            z_copy(h, s, me).wait_send()
         s3_copy(s).wait_send()
 
 
@@ -603,7 +611,7 @@
             vmem((p_rows, depth), bf16),
             vmem((depth, width), bf16),
             vmem((rows, width), f32),
-            vmem((queries, width), bf16),
+            vmem((2, queries, width // 2), bf16),
             vmem((p_rows, width), f32),
             vmem((p_rows, width), bf16),
             vmem((p_rows, width), bf16),
@@ -634,11 +642,9 @@
             dma((w_parts + 2,)),
             dma((6,)),
             dma((2, 2)),
-            dma((2, na)),
-            dma((2, na)),
-            dma((2, na)),
-            dma((2, na)),
-            dma((2, na)),
+            dma((2, 2, na)),
+            dma((2, 2, na)),
+            dma((2, 2, na, 2)),
             dma((2, n)),
             dma((2, n)),
             dma((2, n)),

time: 58.8 us -> 62.6 us (1.065)
  Pallas kernels: 58 us -> 61.7 us
    pallas_call x1, Pallas kernels: 55.9 us -> 59.7 us  [per_device(): pl.pallas_call(functools.partial(kernel, n, names), out_shape=(jax.ShapeD...]
where the time goes in v6:
time: 62.6 us; the launch traced here: 62.4 us
  Pallas kernels  61.7 us (99%)
  between operations  0.64 us (1%)
    pallas_call x1, Pallas kernels, per_device(): pl.pallas_call(functools.partial(kernel, n, names), out_shape=(jax.ShapeD...  59.7 us
    pallas_call x1, Pallas kernels, per_device(): pl.pallas_call(hand_over, out_shape=tuple((jax.ShapeDtypeStruct(x.shape,...  2.06 us

profile of v6, /device:TPU:0, one launch (start us, length us, event | category | flops | bytes accessed | tf_op | source)
XLA Modules:
  0.0 62.4 jit_solution(17997439747732507902)
XLA Ops:
  0.6 59.7 %contrastive.1 = (f32[1,32]{1,0:T(1,128)}, bf16[32,2048]{1,0:T(8,128)(2,1)}, bf16[256,2048]{1,0:T(8,128)(2,1)}) custom-call(bf16[32,4096]{1,0:T(8,128)(2,1)} %q_hbm.1, bf16[256,4096]{1,0:T(8,128)(2,1)} %p_hbm.1, bf16[4096,1024]{1,0:T(8,128)(2,1)} %w_hbm.1, s32[1,32]{1,0:T(1,128)} %bitcast.5, s32[8,32]{1,0:T(8,128)} %bitcast.4, f32[1,32]{1,0:T(1,128)} %bitcast.6), custom_call_target="tpu_custom_call" | custom-call | flops 5637144576 | bytes 12582912 | tf_op jit(solution)/shard_map/contrastive/pallas_call | solution.py:598
  60.3 2.1 %hand_over.1 = (f32[1,32]{1,0:T(1,128)}, bf16[32,2048]{1,0:T(8,128)(2,1)}, bf16[256,2048]{1,0:T(8,128)(2,1)}) custom-call(f32[1,32]{1,0:T(1,128)} %get-tuple-element.9.loss, bf16[32,2048]{1,0:T(8,128)(2,1)} %get-tuple-element.10.q, bf16[256,2048]{1,0:T(8,128)(2,1)} %get-tuple-element.11.p), custom_call_target="tpu_custom_call" | custom-call | tf_op jit(solution)/shard_map/hand_over/pallas_call | solution.py:674

commit v7 on v5

--- a/solution.py
+++ b/solution.py
@@ -54,8 +54,8 @@
     p_proj,
     p_half,
     p_dir,
-    slots,
-    sq_slots,
+    list_z,
+    list_hop,
     lists,
     psq,
     psq_far,
@@ -64,9 +64,9 @@
     raw_far,
     g_q,
     g_p,
-    t_slots,
-    mh,
-    mh_slots,
+    sums_z,
+    sums_hop,
+    sums_all,
     turn,
     part,
     r1,
@@ -87,9 +87,7 @@
     fx_sem,
     fy_sem,
     list_sem,
-    sq_sem,
-    t_sem,
-    mh_sem,
+    sums_sem,
     s1_sem,
     s2_sem,
     s3_sem,
@@ -125,29 +123,41 @@
 
     barrier = pltpu.get_barrier_semaphore()
 
-    @pl.loop(1, n)
-    def _(k):
-        pl.semaphore_signal(
-            barrier,
-            inc=1,
-            device_id={"dp": lax.rem(me + k, n)},
-            device_id_type=pl.DeviceIdType.MESH,
+    def greet(where):
+        pl.semaphore_signal(barrier, inc=1, device_id=where, device_id_type=pl.DeviceIdType.MESH)
+
+    for where in (other, xp, yp):
+        greet(where)
+
+    @pl.loop(1, na)
+    def _(s):
+        greet({"dp": lax.rem(a + s, na) * group + b})
+
+    def hop_copy(hops, sems, k):
+        return remote(
+            hops.at[2 * k], hops.at[2 * k + 1], sems.at[0, na + k], sems.at[1, na + k], (xp, yp)[k]
         )
 
-    pl.semaphore_signal(
-        barrier, inc=1, device_id=other, device_id_type=pl.DeviceIdType.MESH
-    )
-
-    def before(k):
-        return lax.rem(me - k + n, n)
-
-    def list_copy(k, i):
-        to = {"dp": lax.rem(me + k, n)}
-        return remote(slots.at[i], slots.at[i], list_sem.at[0, k], list_sem.at[1, k], to)
-
-    def sq_copy(k, i):
-        to = {"dp": lax.rem(me + k, n)}
-        return remote(sq_slots.at[i], sq_slots.at[i], sq_sem.at[0, k], sq_sem.at[1, k], to)
+    def far_copy(tops, sems, s, i):
+        to = {"dp": lax.rem(a + s, na) * group + b}
+        return remote(tops.at[i], tops.at[i], sems.at[0, s], sems.at[1, s], to)
+
+    def hop_on(hops, tops, sems, k):
+        hop_copy(hops, sems, k).wait_recv()
+        if k == 0:
+            hops[2] = hops[0] + hops[1]
+            hop_copy(hops, sems, 1).start()
+        else:
+            tops[a] = hops[2] + hops[3]
+
+            @pl.loop(1, na)
+            def _(s):
+                far_copy(tops, sems, s, a).start()
+
+    def hop_end(tops, sems):
+        @pl.loop(1, na)
+        def _(s):
+            far_copy(tops, sems, s, lax.rem(a - s + na, na)).wait_recv()
 
     turn[0:24, :] = jnp.zeros((24, tile), f32)
     turn[0 : names - 1, 0:rows] = neg_ref[...].astype(f32)
@@ -158,7 +168,7 @@
     ]
     lane = lax.broadcasted_iota(jnp.int32, (1, tile), 1)
     mask = lane // rows == b
-    slots[me] = jnp.concatenate(
+    list_hop[0] = jnp.concatenate(
         [
             pos_lanes[0:1, :],
             neg_lanes[0 : names - 1, :],
@@ -167,11 +177,7 @@
         ],
         axis=0,
     )
-    pl.semaphore_wait(barrier, n)
-
-    @pl.loop(1, n)
-    def _(k):
-        list_copy(k, me).start()
+    pl.semaphore_wait(barrier, 3 + na - 1)
 
     q_load.wait()
     total = None
@@ -222,11 +228,8 @@
     q_square = jnp.sum(q_proj[...] * q_proj[...], axis=1, keepdims=True)
     square_rows = jnp.broadcast_to(q_square, (rows, tile))
     square_lanes = jnp.concatenate([square_rows] * group, axis=0).T
-    sq_slots[me] = jnp.where(mask, square_lanes[0:1, :], 0.0)
-
-    @pl.loop(1, n)
-    def _(k):
-        sq_copy(k, me).start()
+    list_hop[0, names + 1 : names + 2, :] = jnp.where(mask, square_lanes[0:1, :], 0.0)
+    hop_copy(list_hop, list_sem, 0).start()
 
     p_load.wait()
     p_chunk = 256
@@ -247,6 +250,9 @@
             x_copy(s, column(s)).start()
             y_copy(s, column(s)).start()
 
+        if j < 2:
+            hop_on(list_hop, list_z, list_sem, j)
+
     psq_copy = remote(psq, psq_far, pair.at[0], pair.at[1], other)
     psq_copy.start()
 
@@ -257,20 +263,14 @@
         y_copy(s, column(s) + dy).wait_recv()
         fx_copy(s, column(s) + dy).start()
 
-    @pl.loop(1, n)
-    def _(k):
-        list_copy(k, before(k)).wait_recv()
-        sq_copy(k, before(k)).wait_recv()
+    hop_end(list_z, list_sem)
 
     @pl.loop(0, na)
     def _(t):
         at = pl.ds(pl.multiple_of(t * tile, tile), tile)
-        full, square = slots[t * group], sq_slots[t * group]
-        for g in range(1, group):
-            full = full + slots[t * group + g]
-            square = square + sq_slots[t * group + g]
+        full = list_z[t]
         lists[:, at] = full
-        raw[p_rows : p_rows + 8, at] = jnp.broadcast_to(square, (8, tile))
+        raw[p_rows : p_rows + 8, at] = jnp.broadcast_to(full[names + 1 : names + 2, :], (8, tile))
 
     def strip_of(i):
         return pl.ds(pl.multiple_of(i * strip, strip), strip)
@@ -342,31 +342,13 @@
         sums = lax.fori_loop(i * s_strips, (i + 1) * s_strips, score_strip, sums)
     total, moment, hit = sums
 
-    t_slots[me] = total
-    for t in range(na):
-        at = slice(t * tile, (t + 1) * tile)
-        mh[t] = jnp.concatenate([moment[:, at], hit[:, at], jnp.zeros((6, tile), f32)], axis=0)
-    mh_slots[me] = mh[a]
-
-    def t_copy(k, i):
-        to = {"dp": lax.rem(me + k, n)}
-        return remote(t_slots.at[i], t_slots.at[i], t_sem.at[0, k], t_sem.at[1, k], to)
-
-    def mh_copy(k, i):
-        peer = lax.rem(me + k, n)
-        return remote(
-            mh.at[peer // group], mh_slots.at[i], mh_sem.at[0, k], mh_sem.at[1, k], {"dp": peer}
-        )
-
-    @pl.loop(1, n)
-    def _(k):
-        t_copy(k, me).start()
-
-    @pl.loop(1, n)
-    def _(k):
-        t_copy(k, before(k)).wait_recv()
-
-    total = lax.fori_loop(0, n, lambda i, s: s + t_slots[i], zero)
+    sums_hop[0] = jnp.concatenate([total, moment, hit, zero], axis=0)
+    hop_copy(sums_hop, sums_sem, 0).start()
+    hop_on(sums_hop, sums_z, sums_sem, 0)
+    hop_on(sums_hop, sums_z, sums_sem, 1)
+    hop_end(sums_z, sums_sem)
+    sums_all[...] = lax.fori_loop(1, na, lambda i, t: t + sums_z[i], sums_z[0])
+    total = sums_all[0:1, :]
 
     @pl.loop(0, p_rows // strip)
     def _(i):
@@ -411,10 +393,6 @@
             for h in range(2):
                 s1_copy(s, h, c).start()
 
-    @pl.loop(1, n)
-    def _(k):
-        mh_copy(k, me).start()
-
     for j in range(p_steps):
         at = slice(j * p_chunk, (j + 1) * p_chunk)
         grad = dot(g_p[...], q_all[:, at])
@@ -476,17 +454,9 @@
         p_done[c] = (kept + p_recv[c].astype(f32)).astype(bf16)
         done_copy(c).start()
 
-    @pl.loop(1, n)
-    def _(k):
-        mh_copy(k, before(k)).wait_recv()
-
-    sums = lax.fori_loop(0, n, lambda i, s: s + mh_slots[i], jnp.zeros((8, tile), f32))
     at = pl.ds(pl.multiple_of(a * tile, tile), tile)
-    t_own = lax.fori_loop(
-        0, n, lambda i, s: s + t_slots[i, :, at], jnp.zeros((1, tile), f32)
-    )
+    t_own, own_moment, own_hit = [sums_all[i : i + 1, at] for i in range(3)]
     inv = lax.rsqrt(raw[p_rows : p_rows + 1, at] + raw_far[p_rows : p_rows + 1, at] + 1e-06)
-    own_moment, own_hit = sums[0:1, :], sums[1:2, :]
     loss = jnp.log(t_own) - own_hit
     radial = lists[9:10, at] * (own_moment / t_own - own_hit)
     three = jnp.concatenate([loss, inv, inv * radial, jnp.zeros((5, tile), f32)], axis=0)
@@ -528,12 +498,9 @@
         p_copy(c).wait_send()
         done_copy(c).wait()
 
-    @pl.loop(1, n)
-    def _(k):
-        list_copy(k, me).wait_send()
-        sq_copy(k, me).wait_send()
-        t_copy(k, me).wait_send()
-        mh_copy(k, me).wait_send()
+    for k in range(2):
+        hop_copy(list_hop, list_sem, k).wait_send()
+        hop_copy(sums_hop, sums_sem, k).wait_send()
 
     @pl.loop(0, na)
     def _(s):
@@ -549,6 +516,8 @@
     @pl.loop(1, na)
     def _(s):
         z_copy(s, me).wait_send()
+        far_copy(list_z, list_sem, s, a).wait_send()
+        far_copy(sums_z, sums_sem, s, a).wait_send()
         s3_copy(s).wait_send()
 
 
@@ -607,8 +576,8 @@
             vmem((p_rows, width), f32),
             vmem((p_rows, width), bf16),
             vmem((p_rows, width), bf16),
-            vmem((n, 16, tile), f32),
-            vmem((n, 1, tile), f32),
+            vmem((na, 16, tile), f32),
+            vmem((4, 16, tile), f32),
             vmem((16, queries), f32),
             vmem((p_rows, tile), f32),
             vmem((p_rows, tile), f32),
@@ -617,9 +586,9 @@
             vmem((p_rows + 8, queries), f32),
             vmem((p_rows, queries), bf16),
             vmem((p_rows, queries), bf16),
-            vmem((n, 1, queries), f32),
-            vmem((na, 8, tile), f32),
-            vmem((n, 8, tile), f32),
+            vmem((na, 4, queries), f32),
+            vmem((4, 4, queries), f32),
+            vmem((4, queries), f32),
             vmem((tile, tile), f32),
             vmem((queries, width), bf16),
             vmem((na, 2, 2, piece, width), bf16),
@@ -639,10 +608,8 @@
             dma((2, na)),
             dma((2, na)),
             dma((2, na)),
-            dma((2, n)),
-            dma((2, n)),
-            dma((2, n)),
-            dma((2, n)),
+            dma((2, na + 2)),
+            dma((2, na + 2)),
             dma((2, na, 4)),
             dma((2, na, 2)),
             dma((2, na)),

time: 58.8 us -> 58.1 us (0.988)
  Pallas kernels: 58 us -> 57.3 us
    pallas_call x1, Pallas kernels: 55.9 us -> 55.2 us  [per_device(): pl.pallas_call(functools.partial(kernel, n, names), out_shape=(jax.ShapeD...]
where the time goes in v7:
time: 58.1 us; the launch traced here: 57.9 us
  Pallas kernels  57.3 us (99%)
  between operations  0.64 us (1%)
    pallas_call x1, Pallas kernels, per_device(): pl.pallas_call(functools.partial(kernel, n, names), out_shape=(jax.ShapeD...  55.2 us
    pallas_call x1, Pallas kernels, per_device(): pl.pallas_call(hand_over, out_shape=tuple((jax.ShapeDtypeStruct(x.shape,...  2.06 us

profile of v7, /device:TPU:0, one launch (start us, length us, event | category | flops | bytes accessed | tf_op | source)
XLA Modules:
  0.0 57.9 jit_solution(4437445612704733418)
XLA Ops:
  0.6 55.2 %contrastive.1 = (f32[1,32]{1,0:T(1,128)}, bf16[32,2048]{1,0:T(8,128)(2,1)}, bf16[256,2048]{1,0:T(8,128)(2,1)}) custom-call(bf16[32,4096]{1,0:T(8,128)(2,1)} %q_hbm.1, bf16[256,4096]{1,0:T(8,128)(2,1)} %p_hbm.1, bf16[4096,1024]{1,0:T(8,128)(2,1)} %w_hbm.1, s32[1,32]{1,0:T(1,128)} %bitcast.5, s32[8,32]{1,0:T(8,128)} %bitcast.4, f32[1,32]{1,0:T(1,128)} %bitcast.6), custom_call_target="tpu_custom_call" | custom-call | flops 5637144576 | bytes 12582912 | tf_op jit(solution)/shard_map/contrastive/pallas_call | solution.py:559
  55.8 2.1 %hand_over.1 = (f32[1,32]{1,0:T(1,128)}, bf16[32,2048]{1,0:T(8,128)(2,1)}, bf16[256,2048]{1,0:T(8,128)(2,1)}) custom-call(f32[1,32]{1,0:T(1,128)} %get-tuple-element.9.loss, bf16[32,2048]{1,0:T(8,128)(2,1)} %get-tuple-element.10.q, bf16[256,2048]{1,0:T(8,128)(2,1)} %get-tuple-element.11.p), custom_call_target="tpu_custom_call" | custom-call | tf_op jit(solution)/shard_map/hand_over/pallas_call | solution.py:635
